TPU v7x, 32 devices: a whole 2x2x4 slice. The times are simulated.
32 devices in a mesh: section: 2 (over core), seq: 4 (over z), wa: 4 (over y, x).
Axes of the slice: x: 2, y: 2, z: 4, core: 2. Of those that a mesh axis runs over, the one named last changes fastest.
Arguments:
- tokens: bfloat16 [2, 4, 2048, 1024], P(None, 'wa', 'seq'), may hold values from -6 to 6
- cotangent: bfloat16 [2, 4, 2048, 1024], P(None, 'wa', 'seq'), may hold values from -6 to 6
- input_gain: bfloat16 [2, 1024], P('section', 'wa'), may hold values from 0.25 to 1.75
- gate_proj: bfloat16 [2, 1024, 2048], P('section', 'wa'), may hold values from -0.1875 to 0.1875
- mixed_proj: bfloat16 [2, 1024, 2304], P('section', 'wa'), may hold values from -0.1875 to 0.1875
- step_proj: bfloat16 [2, 1024, 32], P('section', 'wa'), may hold values from -0.1875 to 0.1875
- conv_kernel: bfloat16 [2, 4, 2304], P('section', None, 'wa'), may hold values from -3 to 3
- conv_bias: bfloat16 [2, 2304], P('section', 'wa'), may hold values from -3 to 3
- step_bias: bfloat16 [2, 32], P('section', 'wa'), may hold values from -16 to -2, as said below
- decay_log: bfloat16 [2, 32], P('section', 'wa'), may hold values from 0 to 1.1953125
- skip_gain: bfloat16 [2, 32], P('section', 'wa'), may hold values from 0.5 to 1.5
- output_gain: bfloat16 [2, 2048], P('section', 'wa'), may hold values from 0.25 to 1.75
- out_proj: bfloat16 [2, 2048, 1024], P('section', 'wa'), may hold values from -0.125 to 0.125
Outputs:
- layer_out: bfloat16 [2, 2, 4, 2048, 1024], P('section', None, 'wa', 'seq')
- input_grad: float32 [2, 2, 4, 2048, 1024], P('section', None, 'wa', 'seq')
- input_gain_grad: float32 [2, 1024], P('section', 'wa')
- gate_proj_grad: float32 [2, 1024, 2048], P('section', 'wa')
- mixed_proj_grad: float32 [2, 1024, 2304], P('section', 'wa')
- step_proj_grad: float32 [2, 1024, 32], P('section', 'wa')
- conv_kernel_grad: float32 [2, 4, 2304], P('section', None, 'wa')
- conv_bias_grad: float32 [2, 2304], P('section', 'wa')
- step_bias_grad: float32 [2, 32], P('section', 'wa')
- decay_log_grad: float32 [2, 32], P('section', 'wa')
- skip_gain_grad: float32 [2, 32], P('section', 'wa')
- output_gain_grad: float32 [2, 2048], P('section', 'wa')
- out_proj_grad: float32 [2, 2048, 1024], P('section', 'wa')
Inputs may be any that keep to these rules, and one draw needn't show every extreme that they name: `step_bias`: a per-head number; softplus of it lies between about 0.02 / 2048 and about 0.05.
All inputs are finite; a program needn't handle non-finite values.
Results may differ from a plain program's by a relative error of at most 0.035.
Values may be sent and summed in bfloat16 or wider, within the bound.
A program may use at most 448 MiB of HBM per device.

v0:
```python
import jax
import jax.numpy as jnp
from jax import lax
from jax.sharding import PartitionSpec as P

HEADDIM = 64
GROUP = 256


EPSILON = 1e-05
HIGHEST = lax.Precision.HIGHEST


def passed_along(block, axis, distance):
    devices = range(lax.axis_size(axis))
    route = [(i - distance, i) for i in devices if i - distance in devices]
    return lax.ppermute(block, axis, route)


def prefix(part, axis, combine, identity):
    place = lax.axis_index(axis)
    gathered = jax.tree.map(lambda a: lax.all_gather(a, axis), part)
    state = jax.tree.map(lambda a, e: jnp.zeros_like(a) + jnp.asarray(e, a.dtype), part, identity)

    def prefix_one(step, state):
        return combine(
            state, jax.tree.map(lambda a: lax.dynamic_index_in_dim(a, step, 0, False), gathered)
        )

    return lax.fori_loop(0, place, prefix_one, state)


def carried_in(shard, axis, join, neutral):
    count = lax.axis_size(axis)
    place = lax.axis_index(axis)
    ahead = count - 1 - place
    gathered = jax.tree.map(
        lambda a, kind: lax.all_gather(a.astype(kind), axis),
        shard,
        jax.tree.map(lambda a: jnp.bfloat16 if a.dtype == jnp.float32 else a.dtype, shard),
    )
    state = jax.tree.map(lambda a, e: jnp.zeros_like(a) + jnp.asarray(e, a.dtype), shard, neutral)

    def carried_one(step, state):
        source = count - 1 - step
        return join(
            state,
            jax.tree.map(
                lambda a, own: lax.dynamic_index_in_dim(a, source, 0, False).astype(own.dtype),
                gathered,
                shard,
            ),
        )

    return lax.fori_loop(0, ahead, carried_one, state)


def as_sent(shard):
    return jax.tree.map(lambda a: a.astype(jnp.bfloat16) if a.dtype == jnp.float32 else a, shard)


def rms_scale(values, gain):
    return values * lax.rsqrt(jnp.mean(values * values, axis=-1, keepdims=True) + EPSILON) * gain


def expand_heads(decays):
    return jnp.repeat(decays, HEADDIM, axis=-1)[..., None]


def join_states(earlier, later):
    return (earlier[0] * later[0], earlier[1] * expand_heads(later[0]) + later[1])


def entry_piece(hidden, input_gain):
    return rms_scale(hidden, input_gain)


def conv_piece(extended, step_raw, conv_kernel, conv_bias, step_bias, decay_log):
    length = step_raw.shape[0]
    conv_sum = conv_bias
    for offset in range(conv_kernel.shape[0]):
        conv_sum = conv_sum + conv_kernel[offset] * extended[offset : offset + length]
    time_step = jax.nn.softplus(step_raw + step_bias)
    return (jax.nn.silu(conv_sum), time_step, -jnp.exp(decay_log) * time_step)


def block_piece(log_decay, time_step, values, keys_in, queries):
    length = log_decay.shape[0]
    cumulative = jnp.cumsum(log_decay, axis=0)
    gram_mat = jnp.einsum("tn,sn->ts", queries, keys_in, precision=HIGHEST)
    by_head = cumulative.T
    spread = by_head[:, :, None] - by_head[:, None, :]
    lower_mask = (jnp.arange(length)[:, None] >= jnp.arange(length)[None, :])[None]
    decay_mat = jnp.where(lower_mask, jnp.exp(jnp.where(lower_mask, spread, 0.0)), 0.0)
    mixing = gram_mat[None] * decay_mat * time_step.T[:, None, :]
    weight = jnp.exp(cumulative[-1:] - cumulative) * time_step
    scaled = values * jnp.repeat(weight, HEADDIM, axis=1)
    fresh_state = jnp.einsum("sd,sn->dn", scaled, keys_in, precision=HIGHEST)
    return (mixing, fresh_state, jnp.exp(cumulative[-1]), jnp.exp(cumulative))


def reach_piece(growth, queries, start_state):
    reach_mat = jnp.einsum("tn,dn->td", queries, start_state, precision=HIGHEST)
    return reach_mat * jnp.repeat(growth, HEADDIM, axis=1)


def own_piece(fresh_all, decay_all):
    own_state = jnp.zeros_like(fresh_all[0])
    own_decay = jnp.ones_like(decay_all[0])
    prefixes = []
    prefix_decay = []
    for block_index in range(fresh_all.shape[0]):
        prefixes.append(own_state)
        prefix_decay.append(own_decay)
        own_state = own_state * expand_heads(decay_all[block_index]) + fresh_all[block_index]
        own_decay = own_decay * decay_all[block_index]
    return (own_state, own_decay, jnp.stack(prefixes), jnp.stack(prefix_decay))


def start_piece(incoming, prefix_decay, prefixes):
    return incoming[None] * expand_heads(prefix_decay) + prefixes


def exit_piece(inner_all, outer_all, values, skip_gain, gate_pre, output_gain):
    mixed_out = inner_all + outer_all + values * jnp.repeat(skip_gain, HEADDIM)
    return rms_scale(mixed_out * jax.nn.silu(gate_pre), output_gain)


def fetch(shards):
    whole = (
        lax.all_gather(shards[0], "wa", axis=1, tiled=True),
        lax.all_gather(shards[1], "wa", axis=1, tiled=True),
        lax.all_gather(shards[2], "wa", axis=1, tiled=True),
        lax.all_gather(shards[3], "wa", axis=1, tiled=True),
        lax.all_gather(shards[4], "wa", axis=2, tiled=True),
        lax.all_gather(shards[5], "wa", axis=1, tiled=True),
        lax.all_gather(shards[6], "wa", axis=1, tiled=True),
        lax.all_gather(shards[7], "wa", axis=1, tiled=True),
        lax.all_gather(shards[8], "wa", axis=1, tiled=True),
        lax.all_gather(shards[9], "wa", axis=1, tiled=True),
        lax.all_gather(shards[10], "wa", axis=1, tiled=True),
    )
    return tuple((piece[0] for piece in whole))


def share_out(grads):
    return (
        lax.psum_scatter(
            grads[0][None].astype(jnp.bfloat16), "wa", scatter_dimension=1, tiled=True
        ).astype(jnp.float32),
        lax.psum_scatter(
            grads[1][None].astype(jnp.bfloat16), "wa", scatter_dimension=1, tiled=True
        ).astype(jnp.float32),
        lax.psum_scatter(
            grads[2][None].astype(jnp.bfloat16), "wa", scatter_dimension=1, tiled=True
        ).astype(jnp.float32),
        lax.psum_scatter(
            grads[3][None].astype(jnp.bfloat16), "wa", scatter_dimension=1, tiled=True
        ).astype(jnp.float32),
        lax.psum_scatter(
            grads[4][None].astype(jnp.bfloat16), "wa", scatter_dimension=2, tiled=True
        ).astype(jnp.float32),
        lax.psum_scatter(
            grads[5][None].astype(jnp.bfloat16), "wa", scatter_dimension=1, tiled=True
        ).astype(jnp.float32),
        lax.psum_scatter(
            grads[6][None].astype(jnp.bfloat16), "wa", scatter_dimension=1, tiled=True
        ).astype(jnp.float32),
        lax.psum_scatter(
            grads[7][None].astype(jnp.bfloat16), "wa", scatter_dimension=1, tiled=True
        ).astype(jnp.float32),
        lax.psum_scatter(
            grads[8][None].astype(jnp.bfloat16), "wa", scatter_dimension=1, tiled=True
        ).astype(jnp.float32),
        lax.psum_scatter(
            grads[9][None].astype(jnp.bfloat16), "wa", scatter_dimension=1, tiled=True
        ).astype(jnp.float32),
        lax.psum_scatter(
            grads[10][None].astype(jnp.bfloat16), "wa", scatter_dimension=1, tiled=True
        ).astype(jnp.float32),
    )


def layer_pass(hidden, params, rim_given=None, incoming_given=None):
    (
        input_gain,
        gate_proj,
        mixed_proj,
        step_proj,
        conv_kernel,
        conv_bias,
        step_bias,
        decay_log,
        skip_gain,
        output_gain,
        out_proj,
    ) = params
    length = hidden.shape[0]
    inner_width = gate_proj.shape[1]
    state_width = (mixed_proj.shape[1] - inner_width) // 2
    head_count = step_proj.shape[1]
    block_count = length // GROUP
    rim_rows = conv_kernel.shape[0] - 1
    normed, entry_back = jax.vjp(entry_piece, hidden, input_gain.astype(jnp.float32))
    normed_low = normed.astype(jnp.bfloat16)
    gate_pre = jnp.dot(normed_low, gate_proj, preferred_element_type=jnp.float32)
    mixed_low = jnp.dot(normed_low, mixed_proj, preferred_element_type=jnp.float32).astype(
        jnp.bfloat16
    )
    step_raw = jnp.dot(normed_low, step_proj, preferred_element_type=jnp.float32)
    rim_in = passed_along(mixed_low[length - rim_rows :], "seq", 1)
    extended = jnp.concatenate([rim_in, mixed_low], axis=0).astype(jnp.float32)
    conv_out, conv_back = jax.vjp(
        conv_piece,
        extended,
        step_raw,
        conv_kernel.astype(jnp.float32),
        conv_bias.astype(jnp.float32),
        step_bias.astype(jnp.float32),
        decay_log.astype(jnp.float32),
    )
    active, time_step, log_decay = conv_out
    active_low = active.astype(jnp.bfloat16)
    active_up = active_low.astype(jnp.float32)
    values_low = active_low[:, :inner_width]
    values_up = active_up[:, :inner_width]
    keys_up = active_up[:, inner_width : inner_width + state_width]
    queries_up = active_up[:, inner_width + state_width :]
    inner_parts = []
    mixing_list = []
    block_backs = []
    fresh_list = []
    decay_list = []
    growth_list = []
    for block_index in range(block_count):
        row_span = slice(block_index * GROUP, (block_index + 1) * GROUP)
        outputs, block_back = jax.vjp(
            block_piece,
            log_decay[row_span],
            time_step[row_span],
            values_up[row_span],
            keys_up[row_span],
            queries_up[row_span],
        )
        mixing_low = outputs[0].astype(jnp.bfloat16)
        heads_view = values_low[row_span].reshape(GROUP, head_count, HEADDIM)
        inner_parts.append(
            jnp.einsum(
                "hts,shp->thp", mixing_low, heads_view, preferred_element_type=jnp.float32
            ).reshape(GROUP, inner_width)
        )
        mixing_list.append(mixing_low)
        block_backs.append(block_back)
        fresh_list.append(outputs[1])
        decay_list.append(outputs[2])
        growth_list.append(outputs[3])
    own_out, own_back = jax.vjp(own_piece, jnp.stack(fresh_list), jnp.stack(decay_list))
    own_state, own_decay, prefixes, prefix_decay = own_out
    identity = (jnp.ones_like(own_decay), jnp.zeros_like(own_state))
    incoming = prefix((own_decay, own_state), "seq", join_states, identity)[1]
    starts, start_back = jax.vjp(start_piece, incoming, prefix_decay, prefixes)
    outer_parts = []
    reach_backs = []
    for block_index in range(block_count):
        row_span = slice(block_index * GROUP, (block_index + 1) * GROUP)
        outer_part, reach_back = jax.vjp(
            reach_piece, growth_list[block_index], queries_up[row_span], starts[block_index]
        )
        outer_parts.append(outer_part)
        reach_backs.append(reach_back)
    inner_all = jnp.concatenate(inner_parts, axis=0)
    outer_all = jnp.concatenate(outer_parts, axis=0)
    normed_out, exit_back = jax.vjp(
        exit_piece,
        inner_all,
        outer_all,
        values_up,
        skip_gain.astype(jnp.float32),
        gate_pre,
        output_gain.astype(jnp.float32),
    )
    normed_out_low = normed_out.astype(jnp.bfloat16)
    result = hidden + jnp.dot(normed_out_low, out_proj, preferred_element_type=jnp.float32)
    tape = (
        normed_low,
        entry_back,
        conv_back,
        values_low,
        mixing_list,
        block_backs,
        own_back,
        own_decay,
        incoming,
        start_back,
        reach_backs,
        exit_back,
        normed_out_low,
    )
    return (result, tape, (rim_in, incoming))


def layer_back(grad_out, params, tape):
    (
        input_gain,
        gate_proj,
        mixed_proj,
        step_proj,
        conv_kernel,
        conv_bias,
        step_bias,
        decay_log,
        skip_gain,
        output_gain,
        out_proj,
    ) = params
    (
        normed_low,
        entry_back,
        conv_back,
        values_low,
        mixing_list,
        block_backs,
        own_back,
        own_decay,
        incoming,
        start_back,
        reach_backs,
        exit_back,
        normed_out_low,
    ) = tape
    length = grad_out.shape[0]
    inner_width = gate_proj.shape[1]
    head_count = step_proj.shape[1]
    block_count = length // GROUP
    rim_rows = conv_kernel.shape[0] - 1
    grad_proj = grad_out.astype(jnp.bfloat16)
    out_proj_grad = jnp.einsum(
        "te,td->ed", normed_out_low, grad_proj, preferred_element_type=jnp.float32
    )
    grad_normed_out = jnp.einsum(
        "td,ed->te", grad_proj, out_proj, preferred_element_type=jnp.float32
    )
    grad_inner, grad_outer, grad_values_skip, skip_gain_grad, grad_gate_pre, output_gain_grad = (
        exit_back(grad_normed_out)
    )
    grad_inner_low = grad_inner.astype(jnp.bfloat16)
    grad_mixings = []
    grad_values_inner = []
    grad_growths = []
    grad_queries_outer = []
    grad_starts = []
    for block_index in range(block_count):
        row_span = slice(block_index * GROUP, (block_index + 1) * GROUP)
        grad_heads = grad_inner_low[row_span].reshape(GROUP, head_count, HEADDIM)
        heads_view = values_low[row_span].reshape(GROUP, head_count, HEADDIM)
        grad_mixings.append(
            jnp.einsum("thp,shp->hts", grad_heads, heads_view, preferred_element_type=jnp.float32)
        )
        grad_values_inner.append(
            jnp.einsum(
                "hts,thp->shp",
                mixing_list[block_index],
                grad_heads,
                preferred_element_type=jnp.float32,
            ).reshape(GROUP, inner_width)
        )
        grad_growth, grad_query, grad_start = reach_backs[block_index](grad_outer[row_span])
        grad_growths.append(grad_growth)
        grad_queries_outer.append(grad_query)
        grad_starts.append(grad_start)
    grad_incoming, grad_prefix_decay, grad_prefixes = start_back(jnp.stack(grad_starts))
    identity = (jnp.ones_like(own_decay), jnp.zeros_like(grad_incoming))
    returned = carried_in((own_decay, grad_incoming), "seq", join_states, identity)[1]
    grad_own_decay = jnp.sum(returned * incoming, axis=1).reshape(head_count, HEADDIM).sum(axis=1)
    grad_fresh, grad_decays = own_back((returned, grad_own_decay, grad_prefixes, grad_prefix_decay))
    grad_log_list = []
    grad_step_list = []
    grad_values_list = []
    grad_keys_list = []
    grad_queries_list = []
    for block_index in range(block_count):
        grad_log, grad_step, grad_values, grad_keys, grad_queries = block_backs[block_index](
            (
                grad_mixings[block_index],
                grad_fresh[block_index],
                grad_decays[block_index],
                grad_growths[block_index],
            )
        )
        grad_log_list.append(grad_log)
        grad_step_list.append(grad_step)
        grad_values_list.append(grad_values + grad_values_inner[block_index])
        grad_keys_list.append(grad_keys)
        grad_queries_list.append(grad_queries + grad_queries_outer[block_index])
    grad_active = jnp.concatenate(
        [
            jnp.concatenate(grad_values_list, axis=0) + grad_values_skip,
            jnp.concatenate(grad_keys_list, axis=0),
            jnp.concatenate(grad_queries_list, axis=0),
        ],
        axis=1,
    )
    (
        grad_extended,
        grad_step_raw,
        conv_kernel_grad,
        conv_bias_grad,
        step_bias_grad,
        decay_log_grad,
    ) = conv_back(
        (
            grad_active,
            jnp.concatenate(grad_step_list, axis=0),
            jnp.concatenate(grad_log_list, axis=0),
        )
    )
    back_rim = passed_along(grad_extended[:rim_rows], "seq", -1)
    grad_mixed = grad_extended[rim_rows:] + jnp.pad(back_rim, ((length - rim_rows, 0), (0, 0)))
    grad_gate_low = grad_gate_pre.astype(jnp.bfloat16)
    grad_mixed_low = grad_mixed.astype(jnp.bfloat16)
    grad_step_low = grad_step_raw.astype(jnp.bfloat16)
    gate_proj_grad = jnp.einsum(
        "td,te->de", normed_low, grad_gate_low, preferred_element_type=jnp.float32
    )
    mixed_proj_grad = jnp.einsum(
        "td,te->de", normed_low, grad_mixed_low, preferred_element_type=jnp.float32
    )
    step_proj_grad = jnp.einsum(
        "td,te->de", normed_low, grad_step_low, preferred_element_type=jnp.float32
    )
    grad_normed = jnp.einsum(
        "te,de->td", grad_gate_low, gate_proj, preferred_element_type=jnp.float32
    )
    grad_normed = grad_normed + jnp.einsum(
        "te,de->td", grad_mixed_low, mixed_proj, preferred_element_type=jnp.float32
    )
    grad_normed = grad_normed + jnp.einsum(
        "te,de->td", grad_step_low, step_proj, preferred_element_type=jnp.float32
    )
    grad_hidden, input_gain_grad = entry_back(grad_normed)
    grads = (
        input_gain_grad,
        gate_proj_grad,
        mixed_proj_grad,
        step_proj_grad,
        conv_kernel_grad,
        conv_bias_grad,
        step_bias_grad,
        decay_log_grad,
        skip_gain_grad,
        output_gain_grad,
        out_proj_grad,
    )
    return (grad_out + grad_hidden, grads)


def on_device(
    tokens,
    cotangent,
    input_gain,
    gate_proj,
    mixed_proj,
    step_proj,
    conv_kernel,
    conv_bias,
    step_bias,
    decay_log,
    skip_gain,
    output_gain,
    out_proj,
):
    shards = (
        input_gain,
        gate_proj,
        mixed_proj,
        step_proj,
        conv_kernel,
        conv_bias,
        step_bias,
        decay_log,
        skip_gain,
        output_gain,
        out_proj,
    )
    section_count = lax.axis_size("section")
    section_rank = lax.axis_index("section")
    micro_count = tokens.shape[0]
    step_count = micro_count + section_count - 1
    zero_rows = jnp.zeros(tokens.shape[2:], jnp.float32)
    inputs = []
    results = []
    rim_list = []
    incoming_list = []
    for step_index in range(step_count):
        params = fetch(shards)
        first_in = tokens[min(step_index, micro_count - 1), 0].astype(jnp.float32)
        arrived = zero_rows
        if step_index > 0:
            arrived = passed_along(results[-1], "section", 1).astype(jnp.float32)
        hidden = jnp.where(section_rank == 0, first_in, arrived)
        result, unused_tape, carried = layer_pass(hidden, params)
        inputs.append(hidden)
        results.append(result.astype(jnp.bfloat16))
        rim_list.append(carried[0])
        incoming_list.append(carried[1])
    result_stack = jnp.stack(results)
    input_stack = jnp.stack(inputs)
    layer_out = jnp.stack(
        [
            lax.dynamic_index_in_dim(result_stack, slot_index + section_rank, keepdims=False)
            for slot_index in range(micro_count)
        ]
    )[None, :, None]
    back_rank = section_count - 1 - section_rank
    own_grads = cotangent[:, 0]
    back_list = []
    totals = None
    for step_index in range(step_count):
        params = fetch(shards)
        micro_index = step_index - back_rank
        valid = jnp.logical_and(micro_index >= 0, micro_index < micro_count).astype(jnp.float32)
        slot_index = jnp.clip(micro_index, 0, micro_count - 1)
        hidden = lax.dynamic_index_in_dim(input_stack, slot_index + section_rank, keepdims=False)
        own_grad = lax.dynamic_index_in_dim(own_grads, slot_index, keepdims=False).astype(
            jnp.float32
        )
        arrived = zero_rows
        if step_index > 0:
            arrived = passed_along(as_sent(back_list[-1]), "section", -1)
        grad_out = jnp.where(section_rank == section_count - 1, own_grad, arrived)
        unused_result, tape, unused_carried = layer_pass(hidden, params)
        grad_in, grads = layer_back(grad_out, params, tape)
        back_list.append(grad_in)
        masked = tuple((item * valid for item in grads))
        if totals is None:
            totals = masked
        else:
            totals = tuple((left + right for left, right in zip(totals, masked)))
    totals = share_out(totals)
    summed = (
        lax.psum(totals[0].astype(jnp.bfloat16), "seq").astype(jnp.float32),
        lax.psum(totals[1].astype(jnp.bfloat16), "seq").astype(jnp.float32),
        lax.psum(totals[2].astype(jnp.bfloat16), "seq").astype(jnp.float32),
        lax.psum(totals[3].astype(jnp.bfloat16), "seq").astype(jnp.float32),
        lax.psum(totals[4].astype(jnp.bfloat16), "seq").astype(jnp.float32),
        lax.psum(totals[5].astype(jnp.bfloat16), "seq").astype(jnp.float32),
        lax.psum(totals[6].astype(jnp.bfloat16), "seq").astype(jnp.float32),
        lax.psum(totals[7].astype(jnp.bfloat16), "seq").astype(jnp.float32),
        lax.psum(totals[8].astype(jnp.bfloat16), "seq").astype(jnp.float32),
        lax.psum(totals[9].astype(jnp.bfloat16), "seq").astype(jnp.float32),
        lax.psum(totals[10].astype(jnp.bfloat16), "seq").astype(jnp.float32),
    )
    back_stack = jnp.stack(back_list)
    input_grad = jnp.stack(
        [
            lax.dynamic_index_in_dim(back_stack, slot_index + back_rank, keepdims=False)
            for slot_index in range(micro_count)
        ]
    )[None, :, None]
    return (
        layer_out,
        input_grad,
        summed[0],
        summed[1],
        summed[2],
        summed[3],
        summed[4],
        summed[5],
        summed[6],
        summed[7],
        summed[8],
        summed[9],
        summed[10],
    )


def solution(mesh):
    placed = (
        P(None, "wa", "seq", None),
        P(None, "wa", "seq", None),
        P("section", "wa"),
        P("section", "wa", None),
        P("section", "wa", None),
        P("section", "wa", None),
        P("section", None, "wa"),
        P("section", "wa"),
        P("section", "wa"),
        P("section", "wa"),
        P("section", "wa"),
        P("section", "wa"),
        P("section", "wa", None),
    )
    return jax.shard_map(
        on_device,
        mesh=mesh,
        in_specs=placed,
        out_specs=(
            P("section", None, "wa", "seq", None),
            P("section", None, "wa", "seq", None),
            P("section", "wa"),
            P("section", "wa", None),
            P("section", "wa", None),
            P("section", "wa", None),
            P("section", None, "wa"),
            P("section", "wa"),
            P("section", "wa"),
            P("section", "wa"),
            P("section", "wa"),
            P("section", "wa"),
            P("section", "wa", None),
        ),
        check_vma=False,
    )
```

profile of v0, /device:TPU:0, one launch (start us, length us, event | category | flops | bytes accessed | tf_op | source)
XLA Modules:
  0.0 1975.0 jit_solution(10910952409556166711)
XLA Ops:
  14.1 12.2 all-reduce.77
  26.3 7.1 all_gather.72
  34.4 20.7 %all_gather.71 = bf16[1,4,2304]{1,0,2:T(2,128)(2,1)S(1)} all-gather(bf16[1,4,576]{1,0,2:T(2,128)(2,1)S(1)} %copy.714), channel_id=1, replica_groups=mesh['section'=2,'seq'=4,'wa'=4] {'wa'}, dimensions={2}, use_global_device_ids=true | all-gather | bytes 23040 | tf_op jit(solution)/shard_map/all_gather | solution.py:135
  56.3 8.2 all_gather.75
  72.3 47.9 %slice_reduce_fusion.3 = (f32[2304]{0:T(1024)S(1)}, f32[2304]{0:T(1024)S(1)}, f32[2304]{0:T(1024)S(1)}, f32[2304]{0:T(1024)S(1)}) fusion(f32[1,4,2304]{1,0,2:T(1,128)S(1)} %convert_element_type.630), kind=kLoop, calls=%fused_computation.519 | loop fusion | bytes 73728 | tf_op jit(solution)/shard_map/jvp()/slice | solution.py:82
  158.6 9.3 all-gather.9
  172.3 8.2 all_gather.82
  205.0 27.5 %all-gather.37.cloned.1.call-done = f32[8192,128]{1,0:T(8,128)} async-done(((f32[2048,128]{1,0:T(8,128)}), f32[8192,128]{1,0:T(8,128)}) %all-gather.37.cloned.1.call-update) | async-done | bytes 4194320 | tf_op jit(solution)/shard_map/all_gather | solution.py:22
  241.5 44.2 %all-gather.33.cloned.1.call-done = bf16[1,1024,2048]{2,1,0:T(8,128)(2,1)} async-done(((bf16[1,256,2048]{2,1,0:T(8,128)(2,1)}), bf16[1,1024,2048]{2,1,0:T(8,128)(2,1)}) %all-gather.33.cloned.1.call-update) | async-done | bytes 4194320 | tf_op jit(solution)/shard_map/all_gather | solution.py:132
  285.7 9.8 multiply_reduce_fusion.38
  295.5 44.6 %all-gather.35.cloned.1.call-done = bf16[1,2048,1024]{2,1,0:T(8,128)(2,1)} async-done(((bf16[1,512,1024]{2,1,0:T(8,128)(2,1)}), bf16[1,2048,1024]{2,1,0:T(8,128)(2,1)}) %all-gather.35.cloned.1.call-update) | async-done | bytes 4194320 | tf_op jit(solution)/shard_map/all_gather | solution.py:141
  340.1 6.0 fusion.202
  394.4 10.3 all-gather.10
  428.6 36.6 %all-gather.39.cloned.1.call-done = f32[8192,128]{1,0:T(8,128)} async-done(((f32[2048,128]{1,0:T(8,128)}), f32[8192,128]{1,0:T(8,128)}) %all-gather.39.cloned.1.call-update) | async-done | bytes 4194320 | tf_op jit(solution)/shard_map/all_gather | solution.py:22
  531.2 12.5 all-gather.13
  552.3 9.1 all-gather.12
  588.1 22.0 %all-gather.43.cloned.1.call-done = f32[8192,128]{0,1:T(8,128)} async-done(((f32[2048,128]{0,1:T(8,128)}), f32[8192,128]{0,1:T(8,128)}) %all-gather.43.cloned.1.call-update) | async-done | bytes 4194320 | tf_op jit(solution)/shard_map/all_gather | solution.py:22
  628.1 8.7 multiply_reduce_fusion.35
  636.9 9.1 multiply_reduce_fusion.26
  646.0 7.6 multiply_reduce_fusion.29
  663.4 6.3 fusion.577
  693.6 6.8 slice_multiply_fusion.45
  711.0 14.9 fusion.71
  764.9 8.8 multiply_reduce_fusion.23
  773.7 7.2 broadcast_multiply_fusion.2
  780.9 6.2 pad_add_fusion.2
  807.0 11.7 multiply_reduce_fusion.41
  852.5 30.7 %fusion.547 = (f32[512,2304]{1,0:T(8,128)}, bf16[512,2304]{1,0:T(8,128)(2,1)}, f32[512,2304]{1,0:T(8,128)}, f32[512,2304]{1,0:T(8,128)}, bf16[512,2304]{1,0:T(8,...) fusion(f32[515,2304]{1,0:T(8,128)} %maximum_convert_fusion.5, ...), kind=kLoop, calls=%fused_computation.1089 | loop fusion | flops 49545216 | bytes 87340032 | tf_op jit(solution)/shard_map/convert_element_type | solution.py:224
  925.4 7.6 all-gather.15
  933.6 10.5 all-gather.16
  944.0 7.6 all-gather.14
  1030.1 22.9 %all-gather.47.cloned.1.call-done = f32[8192,128]{0,1:T(8,128)} async-done(((f32[2048,128]{0,1:T(8,128)}), f32[8192,128]{0,1:T(8,128)}) %all-gather.47.cloned.1.call-update) | async-done | bytes 4194320 | tf_op jit(solution)/shard_map/all_gather | solution.py:22
  1070.3 18.1 multiply_reduce_fusion.31
  1088.4 9.5 multiply_reduce_fusion.25
  1097.9 7.1 multiply_reduce_fusion.28
  1117.6 6.2 fusion.578
  1147.3 6.8 slice_multiply_fusion.37
  1164.8 15.0 fusion.75
  1219.5 8.6 multiply_reduce_fusion.19
  1228.2 7.2 broadcast_multiply_fusion.1
  1235.4 6.3 pad_add_fusion.1
  1262.0 9.6 multiply_reduce_fusion.40
  1280.1 8.3 all-gather.17
  1293.6 7.4 multiply_reduce_fusion.24
  1349.9 6.6 slice_multiply_fusion.29
  1368.5 14.2 fusion.79
  1388.1 6.6 fusion.118
  1424.9 8.6 multiply_reduce_fusion.15
  1433.6 7.1 broadcast_multiply_fusion
  1440.7 6.3 pad_add_fusion
  1473.4 9.9 multiply_reduce_fusion.39
  1513.4 8.5 fusion.188
  1536.7 7.8 fusion.306
  1544.4 7.6 fusion.309
  1552.0 9.9 fusion.12
  1574.4 10.3 all-reduce.76
  1602.5 9.7 all-gather.11
  1623.3 19.2 all-reduce.78
  1647.0 14.2 all-gather.41.cloned.1.call-done
  1666.8 49.0 %reduce-scatter.26.cloned.1.call-done = bf16[1,512,1024]{2,1,0:T(8,128)(2,1)} async-done(((bf16[1,2048,1024]{2,1,0:T(8,128)(2,1)}), bf16[1,512,1024]{2,1,0:T(8,128)(2,1)}) %reduce-scatter.26.cloned.1.call-update) | async-done | bytes 1048592 | tf_op jit(solution)/shard_map/reduce_scatter | solution.py:178
  1715.8 55.7 %reduce-scatter.20.cloned.1.call-done = bf16[1,256,2048]{2,1,0:T(8,128)(2,1)} async-done(((bf16[1,1024,2048]{2,1,0:T(8,128)(2,1)}), bf16[1,256,2048]{2,1,0:T(8,128)(2,1)}) %reduce-scatter.20.cloned.1.call-update) | async-done | bytes 1048592 | tf_op jit(solution)/shard_map/reduce_scatter | solution.py:151
  1771.5 60.2 %reduce-scatter.22.cloned.1.call-done = bf16[1,256,2304]{2,1,0:T(8,128)(2,1)} async-done(((bf16[1,1024,2304]{2,1,0:T(8,128)(2,1)}), bf16[1,256,2304]{2,1,0:T(8,128)(2,1)}) %reduce-scatter.22.cloned.1.call-update) | async-done | bytes 1179664 | tf_op jit(solution)/shard_map/reduce_scatter | solution.py:154
  1834.6 7.6 multiply_reduce_fusion.36
  1848.0 112.5 %all-reduce.82.cloned.1.call-done = (bf16[1,256,2048]{2,1,0:T(8,128)(2,1)}, bf16[1,256,2304]{2,1,0:T(8,128)(2,1)}, bf16[1,512,1024]{2,1,0:T(8,128)(2,1)}) async-done(((bf16[1,256,2048]{2,1,0:T(8,128)(2,1)}, bf16[1,256,2304]{2,1,0:T(8,128)(2,1)}, bf16[1,512,1024]{2,1,0:T(8,128)(2,1)}), (bf16[1,256,2048]{2,1,0:T(8,128)(2,1)}, bf16[1,256,2304]{2,1,0:T(8,128)(2,1)}, ...) | async-done | bytes 3276816 | tf_op jit(solution)/shard_map/psum | solution.py:542
  (1726 shorter events, 922.1 us)
Async XLA Ops:
  7.2 49.1 %copy-start.366 = (bf16[1,256,32]{1,2,0:T(8,128)(2,1)S(1)}, bf16[1,256,32]{1,2,0:T(8,128)(2,1)}, u32[]{:S(2)}) copy-start(bf16[1,256,32]{1,2,0:T(8,128)(2,1)} %param.37) | copy-start | bytes 49156
  7.2 57.3 %copy-start.54 = (bf16[2,1,512,1024]{3,2,1,0:T(8,128)(2,1)S(1)}, bf16[2,1,512,1024]{3,2,1,0:T(8,128)(2,1)}, u32[]{:S(2)}) copy-start(bf16[2,1,512,1024]{3,2,1,0:T(8,128)(2,1)} %param.32) | copy-start | bytes 6291460
  7.2 113.0 %all-gather.31.cloned.1.call-start = ((), (), s32[]{:S(2)}) async-start(), calls=%async_computation.8 | async-start | bytes 5898240 | tf_op jit(solution)/shard_map/all_gather | solution.py:133
  7.9 224.6 %all-gather.37.cloned.1.call-start = ((), (), s32[]{:S(2)}) async-start(), calls=%async_computation.15 | async-start | bytes 5242880 | tf_op jit(solution)/shard_map/all_gather | solution.py:22
  26.3 39.7 %copy-start.416 = (bf16[32]{0:T(256)(128)(2,1)}, bf16[32]{0:T(256)(128)(2,1)S(1)}, u32[]{:S(2)}) copy-start(bf16[32]{0:T(256)(128)(2,1)S(1)} %get-tuple-element.1041) | copy-start | bytes 196
  33.4 455.6 %copy-start.235 = (f32[1,1024]{1,0:T(1,128)}, f32[1,1024]{1,0:T(1,128)S(1)}, u32[]{:S(2)}) copy-start(f32[1,1024]{1,0:T(1,128)S(1)} %mul.2972) | copy-start | bytes 12292
  56.3 435.4 %copy-start.371 = (f32[32]{0:T(128)}, f32[32]{0:T(128)S(1)}, u32[]{:S(2)}) copy-start(f32[32]{0:T(128)S(1)} %add.1176) | copy-start | bytes 388
  64.5 427.2 %copy-start.107 = (bf16[1,1024,32]{1,2,0:T(8,128)(2,1)}, bf16[1,1024,32]{1,2,0:T(8,128)(2,1)S(1)}, u32[]{:S(2)}) copy-start(bf16[1,1024,32]{1,2,0:T(8,128)(2,1)S(1)} %all_gather.75) | copy-start | bytes 196612
  64.9 426.9 %copy-start.367 = (f32[32]{0:T(128)}, f32[32]{0:T(128)S(1)}, u32[]{:S(2)}) copy-start(f32[32]{0:T(128)S(1)} %fusion.470) | copy-start | bytes 388
  72.3 48.0 %copy-start.410 = (f32[512]{0:T(512)S(1)}, f32[512]{0:T(512)}, u32[]{:S(2)}) copy-start(f32[512]{0:T(512)} %copy-done.409) | copy-start | bytes 6148
  120.1 394.5 %copy-start.180 = (f32[2304]{0:T(1024)}, f32[2304]{0:T(1024)S(1)}, u32[]{:S(2)}) copy-start(f32[2304]{0:T(1024)S(1)} %get-tuple-element.899) | copy-start | bytes 27652
  120.1 394.5 %copy-start.183 = (f32[2304]{0:T(1024)}, f32[2304]{0:T(1024)S(1)}, u32[]{:S(2)}) copy-start(f32[2304]{0:T(1024)S(1)} %get-tuple-element.900) | copy-start | bytes 27652
  120.1 394.5 %copy-start.186 = (f32[2304]{0:T(1024)}, f32[2304]{0:T(1024)S(1)}, u32[]{:S(2)}) copy-start(f32[2304]{0:T(1024)S(1)} %get-tuple-element.901) | copy-start | bytes 27652
  120.2 394.5 %copy-start.189 = (f32[2304]{0:T(1024)}, f32[2304]{0:T(1024)S(1)}, u32[]{:S(2)}) copy-start(f32[2304]{0:T(1024)S(1)} %get-tuple-element.902) | copy-start | bytes 27652
  127.1 12.9 collective-permute-start
  130.9 383.8 %copy-start.204 = (f32[2304]{0:T(1024)}, f32[2304]{0:T(1024)S(1)}, u32[]{:S(2)}) copy-start(f32[2304]{0:T(1024)S(1)} %add.1175) | copy-start | bytes 27652
  152.3 133.3 %all-gather.33.cloned.1.call-start = ((), (), s32[]{:S(2)}) async-start(), calls=%async_computation.9 | async-start | bytes 5242880 | tf_op jit(solution)/shard_map/all_gather | solution.py:132
  153.1 187.0 %all-gather.35.cloned.1.call-start = ((), (), s32[]{:S(2)}) async-start(), calls=%async_computation.10 | async-start | bytes 5242880 | tf_op jit(solution)/shard_map/all_gather | solution.py:141
  153.7 311.6 %all-gather.39.cloned.1.call-start = ((), (), s32[]{:S(2)}) async-start(), calls=%async_computation.16 | async-start | bytes 5242880 | tf_op jit(solution)/shard_map/all_gather | solution.py:22
  153.7 267.2 %copy-start.265 = (pred[256,256]{1,0:T(8,128)(4,1)}, pred[256,256]{1,0:T(8,128)(4,1)S(1)}, u32[]{:S(2)}) copy-start(pred[256,256]{1,0:T(8,128)(4,1)S(1)} %iota_compare_fusion) | copy-start | bytes 196612
  153.9 607.8 %copy-start.251 = (f32[2048]{0:T(1024)}, f32[2048]{0:T(1024)S(1)}, u32[]{:S(2)}) copy-start(f32[2048]{0:T(1024)S(1)} %mul.2467) | copy-start | bytes 24580
  180.4 465.5 %copy-start.194 = (f32[1,2048]{1,0:T(1,128)}, f32[1,2048]{1,0:T(1,128)S(1)}, u32[]{:S(2)}) copy-start(f32[1,2048]{1,0:T(1,128)S(1)} %mul.2973) | copy-start | bytes 24580
  235.0 50.7 %copy-start.411 = (f32[512]{0:T(512)S(1)}, f32[512]{0:T(512)}, u32[]{:S(2)}) copy-start(f32[512]{0:T(512)} %copy-done.409) | copy-start | bytes 6148
  346.1 4.0 collective-permute-start.1
  357.6 15.3 collective-permute-start.2
  385.2 225.0 %all-gather.43.cloned.1.call-start = ((), (), s32[]{:S(2)}) async-start(), calls=%async_computation.18 | async-start | bytes 5242880 | tf_op jit(solution)/shard_map/all_gather | solution.py:22
  481.6 4.2 collective-permute-start.3
  493.7 37.3 %copy-start.218 = (f32[256,32]{0,1:T(8,128)}, f32[256,32]{0,1:T(8,128)S(1)}, u32[]{:S(2)}) copy-start(f32[256,32]{0,1:T(8,128)S(1)} %get-tuple-element.1247) | copy-start | bytes 98308
  495.2 35.8 %copy-start.220 = (f32[256,32]{0,1:T(8,128)}, f32[256,32]{0,1:T(8,128)S(1)}, u32[]{:S(2)}) copy-start(f32[256,32]{0,1:T(8,128)S(1)} %get-tuple-element.1245) | copy-start | bytes 98308
  500.4 12.1 collective-permute-start.5
  525.3 209.3 %all-gather.45.cloned.1.call-start = ((), (), s32[]{:S(2)}) async-start(), calls=%async_computation.19 | async-start | bytes 2621440 | tf_op jit(solution)/shard_map/all_gather | solution.py:38
  549.6 34.2 %collective-permute-start.4 = (bf16[3,2304]{1,0:T(4,128)(2,1)S(1)}, bf16[3,2304]{1,0:T(4,128)(2,1)S(1)}, u32[]{:S(2)}, u32[]{:S(2)}) collective-permute-start(bf16[3,2304]{1,0:T(4,128)(2,1)S(1)} %slice.989), channel_id=1, source_target_pairs={{0,4},{4,8},{8,12},{1,5},{5,9},{9,13},{2,6},{6,10},{10,14},{3,7},{... | collective-permute-start | bytes 41480 | tf_op jit(solution)/shard_map/ppermute | solution.py:17
  681.8 331.1 %all-gather.51.cloned.1.call-start = ((), (), s32[]{:S(2)}) async-start(), calls=%async_computation.22 | async-start | bytes 5242880 | tf_op jit(solution)/shard_map/all_gather | solution.py:22
  801.1 5.9 collective-permute-start.6
  822.9 22.5 %collective-permute-start.11 = (bf16[3,2304]{1,0:T(4,128)(2,1)S(1)}, bf16[3,2304]{1,0:T(4,128)(2,1)S(1)}, u32[]{:S(2)}, u32[]{:S(2)}) collective-permute-start(bf16[3,2304]{1,0:T(4,128)(2,1)S(1)} %slice.1083), channel_id=1, source_target_pairs={{0,4},{4,8},{8,12},{1,5},{5,9},{9,13},{2,6},{6,10},{10,14},{3,7},{... | collective-permute-start | bytes 41480 | tf_op jit(solution)/shard_map/ppermute | solution.py:17
  828.3 21.6 %collective-permute-start.8 = (bf16[3,2304]{1,0:T(4,128)(2,1)S(1)}, bf16[3,2304]{1,0:T(4,128)(2,1)S(1)}, u32[]{:S(2)}, u32[]{:S(2)}) collective-permute-start(bf16[3,2304]{1,0:T(4,128)(2,1)S(1)} %slice.1048), channel_id=1, source_target_pairs={{0,4},{4,8},{8,12},{1,5},{5,9},{9,13},{2,6},{6,10},{10,14},{3,7},{... | collective-permute-start | bytes 41480 | tf_op jit(solution)/shard_map/ppermute | solution.py:17
  833.0 66.9 %copy-start.172 = (f32[512,32]{0,1:T(8,128)}, f32[512,32]{0,1:T(8,128)S(1)}, u32[]{:S(2)}) copy-start(f32[512,32]{0,1:T(8,128)S(1)} %get-tuple-element.1285) | copy-start | bytes 196612
  840.3 42.9 %copy-start.33 = (f32[256,2048]{1,0:T(8,128)}, f32[256,2048]{1,0:T(8,128)S(1)}, u32[]{:S(2)}) copy-start(f32[256,2048]{1,0:T(8,128)S(1)} %copy.855) | copy-start | bytes 6291460
  845.3 40.6 %copy-start.256 = (f32[2048]{0:T(1024)}, f32[2048]{0:T(1024)S(1)}, u32[]{:S(2)}) copy-start(f32[2048]{0:T(1024)S(1)} %mul.2789) | copy-start | bytes 24580
  890.5 162.5 %all-gather.47.cloned.1.call-start = ((), (), s32[]{:S(2)}) async-start(), calls=%async_computation.20 | async-start | bytes 5242880 | tf_op jit(solution)/shard_map/all_gather | solution.py:22
  893.0 127.0 %copy-start.238 = (f32[2,2048]{1,0:T(2,128)}, f32[2,2048]{1,0:T(2,128)S(1)}, u32[]{:S(2)}) copy-start(f32[2,2048]{1,0:T(2,128)S(1)} %mul.2795) | copy-start | bytes 49156
  896.6 129.7 %copy-start.23 = (f32[256,2048]{1,0:T(8,128)}, f32[256,2048]{1,0:T(8,128)S(1)}, u32[]{:S(2)}) copy-start(f32[256,2048]{1,0:T(8,128)S(1)} %copy.862) | copy-start | bytes 6291460
  909.8 149.2 %copy-start.240 = (f32[2,2048]{1,0:T(2,128)}, f32[2,2048]{1,0:T(2,128)S(1)}, u32[]{:S(2)}) copy-start(f32[2,2048]{1,0:T(2,128)S(1)} %mul.2692) | copy-start | bytes 49156
  914.4 53.5 %copy-start.258 = (f32[2048]{0:T(1024)}, f32[2048]{0:T(1024)S(1)}, u32[]{:S(2)}) copy-start(f32[2048]{0:T(1024)S(1)} %mul.2686) | copy-start | bytes 24580
  918.8 32.9 %copy-start.125 = (bf16[512,1024]{1,0:T(8,128)(2,1)S(1)}, bf16[512,1024]{1,0:T(8,128)(2,1)}, u32[]{:S(2)}) copy-start(bf16[512,1024]{1,0:T(8,128)(2,1)} %copy-done.124) | copy-start | bytes 3145732
  918.8 32.9 %copy-start.420 = (bf16[1,1024,2048]{2,1,0:T(8,128)(2,1)S(1)}, bf16[1,1024,2048]{2,1,0:T(8,128)(2,1)}, u32[]{:S(2)}) copy-start(bf16[1,1024,2048]{2,1,0:T(8,128)(2,1)} %all-gather.33.cloned.1.call-done) | copy-start | bytes 12582916
  923.9 164.4 %collective-permute-start.7 = (bf16[512,1024]{1,0:T(8,128)(2,1)}, bf16[512,1024]{1,0:T(8,128)(2,1)}, u32[]{:S(2)}, u32[]{:S(2)}) collective-permute-start(bf16[512,1024]{1,0:T(8,128)(2,1)} %get-tuple-element.1082), channel_id=1, source_target_pairs={{16,0},{17,1},{18,2},{19,3},{20,4},{21,5},{22,6},{23,7},{24,8},{25... | collective-permute-start | bytes 3145736 | tf_op jit(solution)/shard_map/ppermute | solution.py:17
  972.5 216.6 %all-gather.49.cloned.1.call-start = ((), (), s32[]{:S(2)}) async-start(), calls=%async_computation.21 | async-start | bytes 2621440 | tf_op jit(solution)/shard_map/all_gather | solution.py:38
  994.4 129.4 %copy-start.226 = (f32[256,256]{1,0:T(8,128)}, f32[256,256]{1,0:T(8,128)S(1)}, u32[]{:S(2)}) copy-start(f32[256,256]{1,0:T(8,128)S(1)} %fusion.405) | copy-start | bytes 786436
  1135.4 259.3 %all-gather.53.cloned.1.call-start = ((), (), s32[]{:S(2)}) async-start(), calls=%async_computation.23 | async-start | bytes 2621440 | tf_op jit(solution)/shard_map/all_gather | solution.py:38
  1256.1 5.9 collective-permute-start.9
  1276.0 17.6 collective-permute-start.10
  1337.8 235.6 %reduce-scatter.34.cloned.1.call-start = ((), (), s32[]{:S(2)}) async-start(), calls=%async_computation.27 | async-start | bytes 655360
  1388.1 224.4 %reduce-scatter.32.cloned.1.call-start = ((), (), s32[]{:S(2)}) async-start(), calls=%async_computation.26 | async-start | bytes 737280
  1467.5 5.9 collective-permute-start.12
  1471.5 149.7 %reduce-scatter.28.cloned.1.call-start = ((), (), s32[]{:S(2)}) async-start(), calls=%async_computation.24 | async-start | bytes 327680
  1484.4 137.7 %reduce-scatter.30.cloned.1.call-start = ((), (), s32[]{:S(2)}) async-start(), calls=%async_computation.25 | async-start | bytes 737280
  1491.9 131.4 %reduce-scatter.24.cloned.1.call-start = ((), (), s32[]{:S(2)}) async-start(), calls=%async_computation.13 | async-start | bytes 81920 | tf_op jit(solution)/shard_map/reduce_scatter | solution.py:157
  1498.9 162.4 %all-gather.41.cloned.1.call-start = ((), (), s32[]{:S(2)}) async-start(), calls=%async_computation.17 | async-start | bytes 5242880 | tf_op jit(solution)/shard_map/all_gather | solution.py:22
  1504.2 211.6 %reduce-scatter.26.cloned.1.call-start = ((), (), s32[]{:S(2)}) async-start(), calls=%async_computation.14 | async-start | bytes 5242880 | tf_op jit(solution)/shard_map/reduce_scatter | solution.py:178
  1522.0 249.5 %reduce-scatter.20.cloned.1.call-start = ((), (), s32[]{:S(2)}) async-start(), calls=%async_computation.11 | async-start | bytes 5242880 | tf_op jit(solution)/shard_map/reduce_scatter | solution.py:151
  1535.5 296.2 %reduce-scatter.22.cloned.1.call-start = ((), (), s32[]{:S(2)}) async-start(), calls=%async_computation.12 | async-start | bytes 5898240 | tf_op jit(solution)/shard_map/reduce_scatter | solution.py:154
  1562.0 398.5 %all-reduce.82.cloned.1.call-start = ((), (), s32[]{:S(2)}) async-start(), calls=%async_computation.28 | async-start | bytes 6553600 | tf_op jit(solution)/shard_map/psum | solution.py:542
  1663.4 168.3 %copy-start.88 = (f32[256,2048]{1,0:T(8,128)S(1)}, f32[256,2048]{1,0:T(8,128)}, u32[]{:S(2)}) copy-start(f32[256,2048]{1,0:T(8,128)} %copy.755) | copy-start | bytes 6291460
  (434 other events, 2993.7 us)
Sparse Core Ops, SparseCore 0:
  9.9 64.5 all-gather.30
  152.4 80.0 all-gather.36
  234.4 51.2 all-gather.32
  287.4 52.6 all-gather.34
  385.3 79.8 all-gather.38
  525.4 84.7 all-gather.42
  681.9 50.2 all-gather.44
  890.6 78.9 all-gather.50
  972.7 80.3 all-gather.46
  1135.5 49.9 all-gather.48
  1337.9 44.7 all-gather.52
  1388.2 23.6 reduce-scatter.33
  1471.6 25.2 reduce-scatter.31
  1499.5 24.0 reduce-scatter.27
  1526.6 25.0 reduce-scatter.29
  1554.3 23.6 reduce-scatter.23
  1579.5 81.7 all-gather.40
  1664.4 51.3 reduce-scatter.25
  1718.7 52.6 reduce-scatter.19
  1774.6 57.0 reduce-scatter.21
  1834.4 125.9 all-reduce.81
where the time goes:
time: 1990 us; the launch traced here: 1980 us
  matrix products  549 us (28%)
  waiting for transfers between devices  503 us (25%)
  local copies, waits for them, and re-layouts  376 us (19%)
  other arithmetic  320 us (16%)
  blocking collectives  171 us (9%)
  starting transfers between devices  31.1 us (2%)
  between operations  23.4 us (1%)
    all_gather x6, waiting for transfers between devices, prefix(): gathered = jax.tree.map(lambda a: lax.all_gather(a, axis), part)  123 us
    psum x1, waiting for transfers between devices, on_device(): lax.psum(totals[1].astype(jnp.bfloat16), 'seq').astype(jnp.float32)  113 us
    dot_general x24, matrix products, reach_piece(): reach_mat = jnp.einsum('tn,dn->td', queries, start_state, precision=HIGHEST)  72.7 us
    dot_general x24, matrix products, block_piece(): fresh_state = jnp.einsum('sd,sn->dn', scaled, keys_in, precision=HIGHEST)  68.9 us
    dot_general x6, matrix products, layer_back(): jnp.einsum('thp,shp->hts', grad_heads, heads_view, preferred_element_type...  62.5 us
    reduce_scatter x1, waiting for transfers between devices, share_out(): lax.psum_scatter(grads[2][None].astype(jnp.bfloat16), 'wa', scatter_dimen...  60.2 us
    dot_general x12, matrix products, layer_pass(): jnp.einsum('hts,shp->thp', mixing_low, heads_view, preferred_element_type...  56.7 us
    all_gather x6, blocking collectives, prefix(): gathered = jax.tree.map(lambda a: lax.all_gather(a, axis), part)  56.5 us
  transfers between devices with their start and end apart: 34, of which 16 were waited for; matrix products, arithmetic and copies ran while one was open for 39% of the time, Pallas kernels for 0%

commit v1 on v0

--- a/solution.py
+++ b/solution.py
@@ -4,59 +4,17 @@
 from jax.sharding import PartitionSpec as P
 
 HEADDIM = 64
-GROUP = 256
+GROUP = 128
 
 
 EPSILON = 1e-05
-HIGHEST = lax.Precision.HIGHEST
+HIGHEST = lax.Precision.DEFAULT
 
 
 def passed_along(block, axis, distance):
     devices = range(lax.axis_size(axis))
     route = [(i - distance, i) for i in devices if i - distance in devices]
     return lax.ppermute(block, axis, route)
-
-
-def prefix(part, axis, combine, identity):
-    place = lax.axis_index(axis)
-    gathered = jax.tree.map(lambda a: lax.all_gather(a, axis), part)
-    state = jax.tree.map(lambda a, e: jnp.zeros_like(a) + jnp.asarray(e, a.dtype), part, identity)
-
-    def prefix_one(step, state):
-        return combine(
-            state, jax.tree.map(lambda a: lax.dynamic_index_in_dim(a, step, 0, False), gathered)
-        )
-
-    return lax.fori_loop(0, place, prefix_one, state)
-
-
-def carried_in(shard, axis, join, neutral):
-    count = lax.axis_size(axis)
-    place = lax.axis_index(axis)
-    ahead = count - 1 - place
-    gathered = jax.tree.map(
-        lambda a, kind: lax.all_gather(a.astype(kind), axis),
-        shard,
-        jax.tree.map(lambda a: jnp.bfloat16 if a.dtype == jnp.float32 else a.dtype, shard),
-    )
-    state = jax.tree.map(lambda a, e: jnp.zeros_like(a) + jnp.asarray(e, a.dtype), shard, neutral)
-
-    def carried_one(step, state):
-        source = count - 1 - step
-        return join(
-            state,
-            jax.tree.map(
-                lambda a, own: lax.dynamic_index_in_dim(a, source, 0, False).astype(own.dtype),
-                gathered,
-                shard,
-            ),
-        )
-
-    return lax.fori_loop(0, ahead, carried_one, state)
-
-
-def as_sent(shard):
-    return jax.tree.map(lambda a: a.astype(jnp.bfloat16) if a.dtype == jnp.float32 else a, shard)
 
 
 def rms_scale(values, gain):
@@ -126,62 +84,47 @@
     return rms_scale(mixed_out * jax.nn.silu(gate_pre), output_gain)
 
 
-def fetch(shards):
-    whole = (
-        lax.all_gather(shards[0], "wa", axis=1, tiled=True),
-        lax.all_gather(shards[1], "wa", axis=1, tiled=True),
-        lax.all_gather(shards[2], "wa", axis=1, tiled=True),
-        lax.all_gather(shards[3], "wa", axis=1, tiled=True),
-        lax.all_gather(shards[4], "wa", axis=2, tiled=True),
-        lax.all_gather(shards[5], "wa", axis=1, tiled=True),
-        lax.all_gather(shards[6], "wa", axis=1, tiled=True),
-        lax.all_gather(shards[7], "wa", axis=1, tiled=True),
-        lax.all_gather(shards[8], "wa", axis=1, tiled=True),
-        lax.all_gather(shards[9], "wa", axis=1, tiled=True),
-        lax.all_gather(shards[10], "wa", axis=1, tiled=True),
-    )
-    return tuple((piece[0] for piece in whole))
-
-
-def share_out(grads):
-    return (
-        lax.psum_scatter(
-            grads[0][None].astype(jnp.bfloat16), "wa", scatter_dimension=1, tiled=True
-        ).astype(jnp.float32),
-        lax.psum_scatter(
-            grads[1][None].astype(jnp.bfloat16), "wa", scatter_dimension=1, tiled=True
-        ).astype(jnp.float32),
-        lax.psum_scatter(
-            grads[2][None].astype(jnp.bfloat16), "wa", scatter_dimension=1, tiled=True
-        ).astype(jnp.float32),
-        lax.psum_scatter(
-            grads[3][None].astype(jnp.bfloat16), "wa", scatter_dimension=1, tiled=True
-        ).astype(jnp.float32),
-        lax.psum_scatter(
-            grads[4][None].astype(jnp.bfloat16), "wa", scatter_dimension=2, tiled=True
-        ).astype(jnp.float32),
-        lax.psum_scatter(
-            grads[5][None].astype(jnp.bfloat16), "wa", scatter_dimension=1, tiled=True
-        ).astype(jnp.float32),
-        lax.psum_scatter(
-            grads[6][None].astype(jnp.bfloat16), "wa", scatter_dimension=1, tiled=True
-        ).astype(jnp.float32),
-        lax.psum_scatter(
-            grads[7][None].astype(jnp.bfloat16), "wa", scatter_dimension=1, tiled=True
-        ).astype(jnp.float32),
-        lax.psum_scatter(
-            grads[8][None].astype(jnp.bfloat16), "wa", scatter_dimension=1, tiled=True
-        ).astype(jnp.float32),
-        lax.psum_scatter(
-            grads[9][None].astype(jnp.bfloat16), "wa", scatter_dimension=1, tiled=True
-        ).astype(jnp.float32),
-        lax.psum_scatter(
-            grads[10][None].astype(jnp.bfloat16), "wa", scatter_dimension=1, tiled=True
-        ).astype(jnp.float32),
-    )
-
-
-def layer_pass(hidden, params, rim_given=None, incoming_given=None):
+def to_other(block):
+    count = lax.axis_size("section")
+    return lax.ppermute(block, "section", [(i, (i + 1) % count) for i in range(count)])
+
+
+def spread_states(state, decay):
+    high = decay.astype(jnp.bfloat16)
+    low = (decay - high.astype(jnp.float32)).astype(jnp.bfloat16)
+    width = state.shape[1]
+    heads = decay.shape[0]
+    row = jnp.concatenate([high, low, jnp.zeros((width - 2 * heads,), jnp.bfloat16)])[None]
+    packed = jnp.concatenate(
+        [state.astype(jnp.bfloat16), row, jnp.zeros((15, width), jnp.bfloat16)], axis=0
+    )
+    gathered = lax.all_gather(packed, "seq")
+    states = gathered[:, : state.shape[0]]
+    parts = gathered[:, state.shape[0], : 2 * heads].astype(jnp.float32)
+    return states, parts[:, :heads] + parts[:, heads:]
+
+
+def carried_from(states, decays, ahead):
+    count = lax.axis_size("seq")
+    place = lax.axis_index("seq")
+    source = jnp.arange(count)[:, None, None]
+    middle = jnp.arange(count)[None, :, None]
+    if ahead:
+        between = jnp.logical_and(middle < source, middle > place)
+        keep = jnp.arange(count) > place
+    else:
+        between = jnp.logical_and(middle > source, middle < place)
+        keep = jnp.arange(count) < place
+    factor = jnp.prod(jnp.where(between, decays[None], 1.0), axis=1)
+    factor = jnp.where(keep[:, None], factor, 0.0)
+    factor = jnp.repeat(factor, HEADDIM, axis=1)
+    total = states[0].astype(jnp.float32) * factor[0][:, None]
+    for index in range(1, count):
+        total = total + states[index].astype(jnp.float32) * factor[index][:, None]
+    return total
+
+
+def layer_pass(hidden, params):
     (
         input_gain,
         gate_proj,
@@ -256,8 +199,8 @@
         growth_list.append(outputs[3])
     own_out, own_back = jax.vjp(own_piece, jnp.stack(fresh_list), jnp.stack(decay_list))
     own_state, own_decay, prefixes, prefix_decay = own_out
-    identity = (jnp.ones_like(own_decay), jnp.zeros_like(own_state))
-    incoming = prefix((own_decay, own_state), "seq", join_states, identity)[1]
+    states_all, decays_all = spread_states(own_state, own_decay)
+    incoming = carried_from(states_all, decays_all, False)
     starts, start_back = jax.vjp(start_piece, incoming, prefix_decay, prefixes)
     outer_parts = []
     reach_backs = []
@@ -289,14 +232,14 @@
         mixing_list,
         block_backs,
         own_back,
-        own_decay,
+        decays_all,
         incoming,
         start_back,
         reach_backs,
         exit_back,
         normed_out_low,
     )
-    return (result, tape, (rim_in, incoming))
+    return (result, tape)
 
 
 def layer_back(grad_out, params, tape):
@@ -321,7 +264,7 @@
         mixing_list,
         block_backs,
         own_back,
-        own_decay,
+        decays_all,
         incoming,
         start_back,
         reach_backs,
@@ -369,8 +312,8 @@
         grad_queries_outer.append(grad_query)
         grad_starts.append(grad_start)
     grad_incoming, grad_prefix_decay, grad_prefixes = start_back(jnp.stack(grad_starts))
-    identity = (jnp.ones_like(own_decay), jnp.zeros_like(grad_incoming))
-    returned = carried_in((own_decay, grad_incoming), "seq", join_states, identity)[1]
+    adjoints = lax.all_gather(grad_incoming.astype(jnp.bfloat16), "seq")
+    returned = carried_from(adjoints, decays_all, True)
     grad_own_decay = jnp.sum(returned * incoming, axis=1).reshape(head_count, HEADDIM).sum(axis=1)
     grad_fresh, grad_decays = own_back((returned, grad_own_decay, grad_prefixes, grad_prefix_decay))
     grad_log_list = []
@@ -452,6 +395,78 @@
         out_proj_grad,
     )
     return (grad_out + grad_hidden, grads)
+
+
+SMALL = ((0, 1), (3, 1), (4, 2), (5, 1), (6, 1), (7, 1), (8, 1), (9, 1))
+LARGE = (2, 1, 10)
+
+
+def fetch_small(shards):
+    flat = jnp.concatenate([shards[at].reshape(-1) for at, _ in SMALL])
+    gathered = lax.all_gather(flat, ("section", "wa"))
+    sections = lax.axis_size("section")
+    count = lax.axis_size("wa")
+    gathered = gathered.reshape(sections, count, -1)
+    layers = []
+    for level in range(sections):
+        whole = {}
+        start = 0
+        for at, axis in SMALL:
+            shape = shards[at].shape[1:]
+            size = shards[at][0].size
+            part = gathered[level, :, start : start + size]
+            start += size
+            part = part.reshape((count,) + shape)
+            if axis == 1:
+                whole[at] = part.reshape((count * shape[0],) + shape[1:])
+            else:
+                whole[at] = jnp.moveaxis(part, 0, 1).reshape((shape[0], count * shape[1]))
+        layers.append(whole)
+    return layers
+
+
+def fetch_large(shards):
+    sections = lax.axis_size("section")
+    rank = lax.axis_index("section")
+    mine = {at: shards[at][0] for at in LARGE}
+    layers = [dict() for _ in range(sections)]
+    for at in LARGE:
+        rows, columns = mine[at].shape
+        cut = mine[at].reshape(sections, rows // sections, columns)
+        pieces = swapped(cut, rank, sections)
+        for level in range(sections):
+            layers[level][at] = lax.all_gather(
+                pieces[level], ("wa", "section"), axis=0, tiled=True
+            )
+    return layers
+
+
+def swapped(cut, rank, sections):
+    got = [None] * sections
+    arrivals = [lax.dynamic_index_in_dim(cut, rank, 0, False)]
+    for hop in range(1, sections):
+        target = lax.rem(rank + hop, sections)
+        block = lax.dynamic_index_in_dim(cut, target, 0, False)
+        arrivals.append(
+            lax.ppermute(block, "section", [(i, (i + hop) % sections) for i in range(sections)])
+        )
+    for level in range(sections):
+        value = arrivals[0]
+        for hop in range(1, sections):
+            value = jnp.where(lax.rem(level + hop, sections) == rank, arrivals[hop], value)
+        got[level] = value
+    return got
+
+
+def scatter_large(grad):
+    return lax.psum_scatter(
+        grad.astype(jnp.bfloat16), ("wa", "section"), scatter_dimension=0, tiled=True
+    )
+
+
+def reduce_small(grads):
+    flat = jnp.concatenate([grads[at].reshape(-1) for at, _ in SMALL])
+    return lax.psum(flat, ("section", "wa", "seq"))
 
 
 def on_device(
@@ -482,96 +497,90 @@
         output_gain,
         out_proj,
     )
-    section_count = lax.axis_size("section")
-    section_rank = lax.axis_index("section")
+    sections = lax.axis_size("section")
+    rank = lax.axis_index("section")
+    wa_rank = lax.axis_index("wa")
     micro_count = tokens.shape[0]
-    step_count = micro_count + section_count - 1
-    zero_rows = jnp.zeros(tokens.shape[2:], jnp.float32)
-    inputs = []
-    results = []
-    rim_list = []
-    incoming_list = []
-    for step_index in range(step_count):
-        params = fetch(shards)
-        first_in = tokens[min(step_index, micro_count - 1), 0].astype(jnp.float32)
-        arrived = zero_rows
-        if step_index > 0:
-            arrived = passed_along(results[-1], "section", 1).astype(jnp.float32)
-        hidden = jnp.where(section_rank == 0, first_in, arrived)
-        result, unused_tape, carried = layer_pass(hidden, params)
-        inputs.append(hidden)
-        results.append(result.astype(jnp.bfloat16))
-        rim_list.append(carried[0])
-        incoming_list.append(carried[1])
-    result_stack = jnp.stack(results)
-    input_stack = jnp.stack(inputs)
-    layer_out = jnp.stack(
-        [
-            lax.dynamic_index_in_dim(result_stack, slot_index + section_rank, keepdims=False)
-            for slot_index in range(micro_count)
-        ]
-    )[None, :, None]
-    back_rank = section_count - 1 - section_rank
-    own_grads = cotangent[:, 0]
-    back_list = []
-    totals = None
-    for step_index in range(step_count):
-        params = fetch(shards)
-        micro_index = step_index - back_rank
-        valid = jnp.logical_and(micro_index >= 0, micro_index < micro_count).astype(jnp.float32)
-        slot_index = jnp.clip(micro_index, 0, micro_count - 1)
-        hidden = lax.dynamic_index_in_dim(input_stack, slot_index + section_rank, keepdims=False)
-        own_grad = lax.dynamic_index_in_dim(own_grads, slot_index, keepdims=False).astype(
-            jnp.float32
-        )
-        arrived = zero_rows
-        if step_index > 0:
-            arrived = passed_along(as_sent(back_list[-1]), "section", -1)
-        grad_out = jnp.where(section_rank == section_count - 1, own_grad, arrived)
-        unused_result, tape, unused_carried = layer_pass(hidden, params)
-        grad_in, grads = layer_back(grad_out, params, tape)
-        back_list.append(grad_in)
-        masked = tuple((item * valid for item in grads))
-        if totals is None:
-            totals = masked
-        else:
-            totals = tuple((left + right for left, right in zip(totals, masked)))
-    totals = share_out(totals)
-    summed = (
-        lax.psum(totals[0].astype(jnp.bfloat16), "seq").astype(jnp.float32),
-        lax.psum(totals[1].astype(jnp.bfloat16), "seq").astype(jnp.float32),
-        lax.psum(totals[2].astype(jnp.bfloat16), "seq").astype(jnp.float32),
-        lax.psum(totals[3].astype(jnp.bfloat16), "seq").astype(jnp.float32),
-        lax.psum(totals[4].astype(jnp.bfloat16), "seq").astype(jnp.float32),
-        lax.psum(totals[5].astype(jnp.bfloat16), "seq").astype(jnp.float32),
-        lax.psum(totals[6].astype(jnp.bfloat16), "seq").astype(jnp.float32),
-        lax.psum(totals[7].astype(jnp.bfloat16), "seq").astype(jnp.float32),
-        lax.psum(totals[8].astype(jnp.bfloat16), "seq").astype(jnp.float32),
-        lax.psum(totals[9].astype(jnp.bfloat16), "seq").astype(jnp.float32),
-        lax.psum(totals[10].astype(jnp.bfloat16), "seq").astype(jnp.float32),
-    )
-    back_stack = jnp.stack(back_list)
-    input_grad = jnp.stack(
-        [
-            lax.dynamic_index_in_dim(back_stack, slot_index + back_rank, keepdims=False)
-            for slot_index in range(micro_count)
-        ]
-    )[None, :, None]
-    return (
-        layer_out,
-        input_grad,
-        summed[0],
-        summed[1],
-        summed[2],
-        summed[3],
-        summed[4],
-        summed[5],
-        summed[6],
-        summed[7],
-        summed[8],
-        summed[9],
-        summed[10],
-    )
+    share = micro_count // sections
+    small = fetch_small(shards)
+    large = fetch_large(shards)
+    params = []
+    for level in range(sections):
+        merged = {**small[level], **large[level]}
+        params.append(tuple(merged[at] for at in range(len(shards))))
+
+    totals = [None] * sections
+    outs = [[None] * share for _ in range(sections)]
+    backs = [[None] * share for _ in range(sections)]
+    for turn in range(share):
+        own = rank * share + turn
+        hidden = lax.dynamic_index_in_dim(tokens[:, 0], own, 0, False).astype(jnp.float32)
+        tapes = []
+        for level in range(sections):
+            result, tape = layer_pass(hidden, params[level])
+            tapes.append(tape)
+            low = result.astype(jnp.bfloat16)
+            outs[level][turn] = low
+            hidden = low.astype(jnp.float32)
+        grad = lax.dynamic_index_in_dim(cotangent[:, 0], own, 0, False).astype(jnp.float32)
+        for level in reversed(range(sections)):
+            grad, grads = layer_back(grad, params[level], tapes[level])
+            backs[level][turn] = grad
+            if totals[level] is None:
+                totals[level] = grads
+            else:
+                totals[level] = tuple(a + b for a, b in zip(totals[level], grads))
+
+    layer_out = gather_micro(outs, rank, sections, share)[None, :, None]
+    input_grad = gather_micro(backs, rank, sections, share)[None, :, None]
+
+    final = {}
+    parts = [None] * sections
+    sums = [None] * sections
+    before = None
+    for level in reversed(range(sections)):
+        scattered = tuple(scatter_large(totals[level][at]) for at in LARGE)
+        if before is not None:
+            scattered, before = lax.optimization_barrier((scattered, before))
+            parts[level + 1] = before
+        before = lax.psum(scattered, "seq")
+        parts[level] = before
+        sums[level] = reduce_small(totals[level])
+    parts = [dict(zip(LARGE, part)) for part in parts]
+    for at in LARGE:
+        stacked = jnp.stack([parts[level][at] for level in range(sections)])
+        got = swapped(stacked, rank, sections)
+        final[at] = jnp.concatenate(got, axis=0).astype(jnp.float32)[None]
+    flat = lax.dynamic_index_in_dim(jnp.stack(sums), rank, 0, False)
+    start = 0
+    for at, axis in SMALL:
+        shape = totals[0][at].shape
+        size = totals[0][at].size
+        whole = flat[start : start + size].reshape(shape)
+        start += size
+        length = shards[at].shape[axis]
+        final[at] = lax.dynamic_slice_in_dim(whole, wa_rank * length, length, axis - 1)[None]
+    return (layer_out, input_grad) + tuple(final[at] for at in range(len(shards)))
+
+
+def gather_micro(values, rank, sections, share):
+    stacked = jnp.stack([jnp.stack(rows) for rows in values])
+    arrivals = [lax.dynamic_index_in_dim(stacked, rank, 0, False)]
+    for hop in range(1, sections):
+        target = lax.rem(rank + hop, sections)
+        block = lax.dynamic_index_in_dim(stacked, target, 0, False).astype(jnp.bfloat16)
+        arrivals.append(
+            lax.ppermute(
+                block, "section", [(i, (i + hop) % sections) for i in range(sections)]
+            ).astype(stacked.dtype)
+        )
+    pieces = []
+    for source in range(sections):
+        value = arrivals[0]
+        for hop in range(1, sections):
+            value = jnp.where(lax.rem(source + hop, sections) == rank, arrivals[hop], value)
+        pieces.append(value)
+    return jnp.concatenate(pieces, axis=0)
 
 
 def solution(mesh):

time: 1990 us -> 1410 us (0.71)
  matrix products: 549 us -> 273 us
  blocking collectives: 171 us -> 0 us
  local copies, waits for them, and re-layouts: 376 us -> 228 us
  waiting for transfers between devices: 503 us -> 620 us
  other arithmetic: 320 us -> 241 us
    psum x1 -> x3, waiting for transfers between devices: 113 us -> 248 us  [the longest x2 137 us: on_device(): before = lax.psum(scattered, 'seq')]
    all_gather x13 -> x0, blocking collectives: 129 us -> none  [the longest x6 56.5 us: prefix(): gathered = jax.tree.map(lambda a: lax.all_gather(a, axis), part)]
    all_gather x12 -> x10, waiting for transfers between devices: 212 us -> 144 us  [the longest x6 130 us: fetch_large(): lax.all_gather(pieces[level], ('wa', 'section'), axis=0, tiled=True)]
    unnamed x25 -> x21, waiting for transfers between devices: 2.2 us -> 53.6 us
    slice x1 -> x2, local copies, waits for them, and re-layouts: 47.9 us -> 0.26 us  [conv_piece(): conv_sum = conv_sum + conv_kernel[offset] * extended[offset:offset + length]]
    dot_general x24, matrix products: 68.9 us -> 26.9 us  [block_piece(): fresh_state = jnp.einsum('sd,sn->dn', scaled, keys_in, precision=HIGHEST)]
    dot_general x12 -> x8, matrix products: 56.7 us -> 17.4 us  [layer_pass(): jnp.einsum('hts,shp->thp', mixing_low, heads_view, preferred_element_type...]
    dot_general x6 -> x8, matrix products: 62.5 us -> 27.1 us  [layer_back(): jnp.einsum('thp,shp->hts', grad_heads, heads_view, preferred_element_type...]
  transfers between devices with their start and end apart: 34 -> 32, of which waited for: 16 -> 18; matrix products, arithmetic and copies ran while one was open for 39% -> 36% of each run, Pallas kernels for 0% -> 0%
where the time goes in v1:
time: 1410 us; the launch traced here: 1400 us
  waiting for transfers between devices  620 us (44%)
  matrix products  273 us (19%)
  other arithmetic  241 us (17%)
  local copies, waits for them, and re-layouts  228 us (16%)
  between operations  20.8 us (1%)
  starting transfers between devices  14.5 us (1%)
    reduce_scatter x6, waiting for transfers between devices, scatter_large(): lax.psum_scatter(grad.astype(jnp.bfloat16), ('wa', 'section'), scatter_di...  168 us
    psum x2, waiting for transfers between devices, on_device(): before = lax.psum(scattered, 'seq')  137 us
    all_gather x6, waiting for transfers between devices, fetch_large(): lax.all_gather(pieces[level], ('wa', 'section'), axis=0, tiled=True)  130 us
    psum x1, waiting for transfers between devices, reduce_small(): return lax.psum(flat, ('section', 'wa', 'seq'))  110 us
    unnamed x21, waiting for transfers between devices  53.6 us
    unnamed x896, local copies, waits for them, and re-layouts  41 us
    dot_general x24, matrix products, reach_piece(): reach_mat = jnp.einsum('tn,dn->td', queries, start_state, precision=HIGHEST)  37.9 us
  transfers between devices with their start and end apart: 32, of which 18 were waited for; matrix products, arithmetic and copies ran while one was open for 36% of the time, Pallas kernels for 0%

profile of v1, /device:TPU:0, one launch (start us, length us, event | category | flops | bytes accessed | tf_op | source)
XLA Modules:
  0.0 1397.9 jit_solution(15608035405046941090)
XLA Ops:
  21.3 52.6 %all-reduce.67.cloned.1.call-done = bf16[94912]{0:T(1024)(128)(2,1)} async-done(((bf16[94912]{0:T(1024)(128)(2,1)}), bf16[94912]{0:T(1024)(128)(2,1)}) %all-reduce.67.cloned.1.call-update) | async-done | bytes 189840
  83.5 31.2 %all-gather.16.cloned.1.call-done = bf16[1024,2304]{1,0:T(8,128)(2,1)} async-done(((bf16[128,2304]{1,0:T(8,128)(2,1)}), bf16[1024,2304]{1,0:T(8,128)(2,1)}) %all-gather.16.cloned.1.call-update) | async-done | bytes 4718608 | tf_op jit(solution)/shard_map/all_gather | solution.py:438
  114.7 5.3 convolution_convert_fusion.3
  122.1 4.0 collective-permute-start.1
  139.5 4.5 fusion.387
  149.6 3.9 concatenate.127
  229.4 4.1 fusion.84
  244.6 12.0 multiply_reduce_fusion.19
  256.7 17.5 %all-gather.20.cloned.1.call-done = bf16[2048,1024]{1,0:T(8,128)(2,1)} async-done(((bf16[256,1024]{1,0:T(8,128)(2,1)}), bf16[2048,1024]{1,0:T(8,128)(2,1)}) %all-gather.20.cloned.1.call-update) | async-done | bytes 4194320 | tf_op jit(solution)/shard_map/all_gather | solution.py:438
  274.2 6.0 fusion.39
  280.3 34.6 %all-gather.22.cloned.1.call-done = bf16[1024,2304]{1,0:T(8,128)(2,1)} async-done(((bf16[128,2304]{1,0:T(8,128)(2,1)}), bf16[1024,2304]{1,0:T(8,128)(2,1)}) %all-gather.22.cloned.1.call-update) | async-done | bytes 4718608 | tf_op jit(solution)/shard_map/all_gather | solution.py:438
  314.9 5.3 convolution_convert_fusion.2
  320.3 3.4 collective-permute-start.4
  336.1 4.7 fusion.382
  347.6 5.0 concatenate.132
  384.3 13.9 all-gather.30.cloned.1.call-done
  400.3 3.4 fusion.97
  403.8 3.6 maximum_add_fusion.3
  417.3 18.3 %all-gather.24.cloned.1.call-done = bf16[1024,2048]{1,0:T(8,128)(2,1)} async-done(((bf16[128,2048]{1,0:T(8,128)(2,1)}), bf16[1024,2048]{1,0:T(8,128)(2,1)}) %all-gather.24.cloned.1.call-update) | async-done | bytes 4194320 | tf_op jit(solution)/shard_map/all_gather | solution.py:438
  435.6 10.5 multiply_reduce_fusion.18
  446.1 28.1 %all-gather.26.cloned.1.call-done = bf16[2048,1024]{1,0:T(8,128)(2,1)} async-done(((bf16[256,1024]{1,0:T(8,128)(2,1)}), bf16[2048,1024]{1,0:T(8,128)(2,1)}) %all-gather.26.cloned.1.call-update) | async-done | bytes 4194320 | tf_op jit(solution)/shard_map/all_gather | solution.py:438
  474.2 7.3 multiply_reduce_fusion.8
  481.8 6.9 multiply_reduce_fusion.9
  526.4 5.5 multiply_reduce_fusion.15
  535.0 5.9 slice_multiply_fusion.14
  573.4 9.6 fusion.66
  587.7 5.9 multiply_reduce_fusion.42
  612.2 5.7 slice_multiply_fusion.22
  621.1 11.5 multiply_reduce_fusion.3
  632.6 7.2 broadcast_multiply_fusion
  639.8 6.3 pad_add_fusion.1
  660.9 3.5 multiply_reduce_fusion.43
  684.7 6.0 fusion.213
  690.7 3.5 fusion.28
  695.1 5.6 multiply_reduce_fusion.10
  701.2 6.2 multiply_reduce_fusion.11
  713.9 3.5 multiply_reduce_fusion.12
  717.7 6.1 convolution_convert_fusion.5
  725.8 6.9 convolution_convert_fusion.4
  760.3 5.2 slice_multiply_fusion.6
  789.1 6.8 fusion.74
  800.8 4.7 convolution_convert_fusion
  806.7 5.8 multiply_reduce_fusion.38
  825.6 4.1 slice_multiply_fusion.30
  837.0 3.4 multiply_reduce_fusion.39
  863.6 3.8 maximum_add_fusion.5
  867.6 12.0 multiply_reduce_fusion.7
  879.7 7.8 broadcast_multiply_fusion.4
  894.0 3.4 pad_add_fusion
  898.8 6.1 fusion.216
  905.7 4.2 fusion.30
  910.8 5.8 convolution_convert_fusion.7
  918.2 7.0 convolution_convert_fusion.6
  925.4 3.4 reduce-scatter.13.cloned.1.call-done
  928.9 5.9 fusion.64
  937.0 7.1 convolution_convert_fusion.1
  952.5 110.3 %all-reduce.69.cloned.1.call-done = (f32[1,47456]{1,0:T(1,128)}, f32[1,47456]{1,0:T(1,128)}) async-done(((f32[1,47456]{1,0:T(1,128)}, f32[1,47456]{1,0:T(1,128)}), (f32[1,47456]{1,0:T(1,128)}, f32[1,47456]{1,0:T(1,128)})) %all-reduce.69.cloned.1.call-update) | async-done | bytes 379664 | tf_op jit(solution)/shard_map/psum | solution.py:469
  1064.4 52.8 %reduce-scatter.9.cloned.1.call-done = bf16[128,2048]{1,0:T(8,128)(2,1)} async-done(((bf16[1024,2048]{1,0:T(8,128)(2,1)}), bf16[128,2048]{1,0:T(8,128)(2,1)}) %reduce-scatter.9.cloned.1.call-update) | async-done | bytes 524304 | tf_op jit(solution)/shard_map/reduce_scatter | solution.py:462
  1117.2 54.9 %reduce-scatter.11.cloned.1.call-done = bf16[256,1024]{1,0:T(8,128)(2,1)} async-done(((bf16[2048,1024]{1,0:T(8,128)(2,1)}), bf16[256,1024]{1,0:T(8,128)(2,1)}) %reduce-scatter.11.cloned.1.call-update) | async-done | bytes 524304 | tf_op jit(solution)/shard_map/reduce_scatter | solution.py:462
  1172.1 74.5 %all-reduce.73.cloned.1.call-done = (bf16[128,2304]{1,0:T(8,128)(2,1)}, bf16[128,2048]{1,0:T(8,128)(2,1)}, bf16[256,1024]{1,0:T(8,128)(2,1)}) async-done(((bf16[128,2304]{1,0:T(8,128)(2,1)}, bf16[128,2048]{1,0:T(8,128)(2,1)}, bf16[256,1024]{1,0:T(8,128)(2,1)}), (bf16[128,2304]{1,0:T(8,128)(2,1)}, bf16[128,2048]{1,0:T(8,128)(2,1)}, bf16[256,1024]{1,0:T(8,128)(2,1)})) %all-reduce.73.cloned.1.call-update) | async-done | bytes 1638416 | tf_op jit(solution)/shard_map/psum | solution.py:546
  1246.6 56.8 %reduce-scatter.7.cloned.1.call-done = bf16[128,2304]{1,0:T(8,128)(2,1)} async-done(((bf16[1024,2304]{1,0:T(8,128)(2,1)}), bf16[128,2304]{1,0:T(8,128)(2,1)}) %reduce-scatter.7.cloned.1.call-update) | async-done | bytes 589840 | tf_op jit(solution)/shard_map/reduce_scatter | solution.py:462
  1309.1 5.9 convert_select_fusion.1
  1315.0 62.8 %all-reduce.71.cloned.1.call-done = (bf16[1,128,2048]{2,1,0:T(8,128)(2,1)}, bf16[1,128,2304]{2,1,0:T(8,128)(2,1)}, bf16[1,256,1024]{2,1,0:T(8,128)(2,1)}) async-done(((bf16[1,128,2048]{2,1,0:T(8,128)(2,1)}, bf16[1,128,2304]{2,1,0:T(8,128)(2,1)}, bf16[1,256,1024]{2,1,0:T(8,128)(2,1)}), (bf16[1,128,2048]{2,1,0:T(8,128)(2,1)}, bf16[1,128,2304]{2,1,0:T(8,128)(2,1)}, ...) | async-done | bytes 1638416 | tf_op jit(solution)/shard_map/psum | solution.py:546
  1378.1 5.0 maximum_bitcast_fusion
  (1516 shorter events, 472.6 us)
Async XLA Ops:
  7.2 66.7 %all-reduce.67.cloned.1.call-start = ((), (), s32[]{:S(2)}) async-start(), calls=%async_computation.22 | async-start | bytes 380928
  8.5 9.6 collective-permute-start
  18.1 96.6 %all-gather.16.cloned.1.call-start = ((), (), s32[]{:S(2)}) async-start(), calls=%async_computation.6 | async-start | bytes 5308416 | tf_op jit(solution)/shard_map/all_gather | solution.py:438
  20.3 207.0 %all-gather.28.cloned.1.call-start = ((), (), s32[]{:S(2)}) async-start(), calls=%async_computation.18 | async-start | bytes 2641920 | tf_op jit(solution)/shard_map/all_gather | solution.py:101
  21.3 93.4 %copy-start.376 = (f32[512]{0:T(512)}, f32[512]{0:T(512)S(1)}, u32[]{:S(2)}) copy-start(f32[512]{0:T(512)S(1)} %fusion.317) | copy-start | bytes 6148
  75.6 39.1 %copy-start.303 = (f32[1,2,4,128]{3,1,2,0:T(2,128)}, f32[1,2,4,128]{3,1,2,0:T(2,128)S(1)}, u32[]{:S(2)}) copy-start(f32[1,2,4,128]{3,1,2,0:T(2,128)S(1)} %copy.966) | copy-start | bytes 12292
  78.7 41.3 %copy-start.139 = (bf16[1024,32]{1,0:T(8,128)(2,1)}, bf16[1024,32]{1,0:T(8,128)(2,1)S(1)}, u32[]{:S(2)}) copy-start(bf16[1024,32]{1,0:T(8,128)(2,1)S(1)} %reshape_reshape_squeeze.6) | copy-start | bytes 196612
  79.8 40.2 %copy-start.169 = (f32[512,32]{0,1:T(8,128)}, f32[512,32]{0,1:T(8,128)S(1)}, u32[]{:S(2)}) copy-start(f32[512,32]{0,1:T(8,128)S(1)} %get-tuple-element.387) | copy-start | bytes 196612
  80.1 39.9 %copy-start.146 = (f32[128,32]{0,1:T(8,128)}, f32[128,32]{0,1:T(8,128)S(1)}, u32[]{:S(2)}) copy-start(f32[128,32]{0,1:T(8,128)S(1)} %copy.781) | copy-start | bytes 49156
  80.5 39.6 %copy-start.156 = (f32[128,32]{0,1:T(8,128)}, f32[128,32]{0,1:T(8,128)S(1)}, u32[]{:S(2)}) copy-start(f32[128,32]{0,1:T(8,128)S(1)} %copy.778) | copy-start | bytes 49156
  80.8 39.2 %copy-start.144 = (f32[128,32]{0,1:T(8,128)}, f32[128,32]{0,1:T(8,128)S(1)}, u32[]{:S(2)}) copy-start(f32[128,32]{0,1:T(8,128)S(1)} %copy.775) | copy-start | bytes 49156
  81.1 38.9 %copy-start.161 = (f32[128,32]{1,0:T(8,128)}, f32[128,32]{1,0:T(8,128)S(1)}, u32[]{:S(2)}) copy-start(f32[128,32]{1,0:T(8,128)S(1)} %reduce_window_sum.78) | copy-start | bytes 49156
  81.2 38.9 %copy-start.148 = (f32[128,32]{0,1:T(8,128)}, f32[128,32]{0,1:T(8,128)S(1)}, u32[]{:S(2)}) copy-start(f32[128,32]{0,1:T(8,128)S(1)} %copy.784) | copy-start | bytes 49156
  82.2 37.9 %copy-start.356 = (f32[32]{0:T(128)}, f32[32]{0:T(128)S(1)}, u32[]{:S(2)}) copy-start(f32[32]{0:T(128)S(1)} %get-tuple-element.428) | copy-start | bytes 388
  82.2 37.9 %copy-start.358 = (f32[32]{0:T(128)}, f32[32]{0:T(128)S(1)}, u32[]{:S(2)}) copy-start(f32[32]{0:T(128)S(1)} %get-tuple-element.426) | copy-start | bytes 388
  82.2 37.9 %copy-start.368 = (f32[32]{0:T(128)}, f32[32]{0:T(128)S(1)}, u32[]{:S(2)}) copy-start(f32[32]{0:T(128)S(1)} %get-tuple-element.427) | copy-start | bytes 388
  82.2 37.9 %copy-start.370 = (f32[32]{0:T(128)}, f32[32]{0:T(128)S(1)}, u32[]{:S(2)}) copy-start(f32[32]{0:T(128)S(1)} %get-tuple-element.487) | copy-start | bytes 388
  82.2 85.6 %copy-start.175 = (f32[1,32]{0,1:T(8,128)}, f32[1,32]{0,1:T(8,128)S(1)}, u32[]{:S(2)}) copy-start(f32[1,32]{0,1:T(8,128)S(1)} %get-tuple-element.257) | copy-start | bytes 388
  122.1 14.8 %collective-permute-start.1 = (bf16[3,2304]{1,0:T(4,128)(2,1)}, bf16[3,2304]{1,0:T(4,128)(2,1)}, u32[]{:S(2)}, u32[]{:S(2)}) collective-permute-start(bf16[3,2304]{1,0:T(4,128)(2,1)} %slice.908), channel_id=1, source_target_pairs={{0,4},{4,8},{8,12},{1,5},{5,9},{9,13},{2,6},{6,10},{10,14},{3,7},{... | collective-permute-start | bytes 41480 | tf_op jit(solution)/shard_map/ppermute | solution.py:17
  146.0 87.6 %copy-start.18 = (f32[2048,128]{1,0:T(8,128)}, f32[2048,128]{1,0:T(8,128)S(1)}, u32[]{:S(2)}) copy-start(f32[2048,128]{1,0:T(8,128)S(1)} %convolution_add_fusion.7) | copy-start | bytes 3145732
  153.6 91.0 %all-gather.18.cloned.1.call-start = ((), (), s32[]{:S(2)}) async-start(), calls=%async_computation.7 | async-start | bytes 4718592 | tf_op jit(solution)/shard_map/all_gather | solution.py:438
  154.8 2.0 collective-permute-start.2
  157.8 116.4 %all-gather.20.cloned.1.call-start = ((), (), s32[]{:S(2)}) async-start(), calls=%async_computation.8 | async-start | bytes 4718592 | tf_op jit(solution)/shard_map/all_gather | solution.py:438
  159.0 2.0 collective-permute-start.3
  163.1 151.8 %all-gather.22.cloned.1.call-start = ((), (), s32[]{:S(2)}) async-start(), calls=%async_computation.9 | async-start | bytes 5308416 | tf_op jit(solution)/shard_map/all_gather | solution.py:438
  170.1 67.1 %copy-start.21 = (f32[128,2048]{1,0:T(8,128)}, f32[128,2048]{1,0:T(8,128)S(1)}, u32[]{:S(2)}) copy-start(f32[128,2048]{1,0:T(8,128)S(1)} %copy.795) | copy-start | bytes 3145732
  173.4 66.2 %copy-start.24 = (f32[128,2048]{1,0:T(8,128)}, f32[128,2048]{1,0:T(8,128)S(1)}, u32[]{:S(2)}) copy-start(f32[128,2048]{1,0:T(8,128)S(1)} %copy.793) | copy-start | bytes 3145732
  181.4 92.9 %copy-start.287 = (f32[1,4,4,128]{3,1,2,0:T(4,128)}, f32[1,4,4,128]{3,1,2,0:T(4,128)S(1)}, u32[]{:S(2)}) copy-start(f32[1,4,4,128]{3,1,2,0:T(4,128)S(1)} %copy.967) | copy-start | bytes 24580
  183.7 152.3 %copy-start.200 = (f32[2304]{0:T(1024)}, f32[2304]{0:T(1024)S(1)}, u32[]{:S(2)}) copy-start(f32[2304]{0:T(1024)S(1)} %mul.1747) | copy-start | bytes 27652
  183.8 152.2 %copy-start.201 = (f32[2304]{0:T(1024)}, f32[2304]{0:T(1024)S(1)}, u32[]{:S(2)}) copy-start(f32[2304]{0:T(1024)S(1)} %mul.1744) | copy-start | bytes 27652
  183.9 152.2 %copy-start.202 = (f32[2304]{0:T(1024)}, f32[2304]{0:T(1024)S(1)}, u32[]{:S(2)}) copy-start(f32[2304]{0:T(1024)S(1)} %mul.1741) | copy-start | bytes 27652
  184.0 152.1 %copy-start.203 = (f32[2304]{0:T(1024)}, f32[2304]{0:T(1024)S(1)}, u32[]{:S(2)}) copy-start(f32[2304]{0:T(1024)S(1)} %mul.1733) | copy-start | bytes 27652
  188.3 135.4 %copy-start.141 = (bf16[1024,32]{1,0:T(8,128)(2,1)}, bf16[1024,32]{1,0:T(8,128)(2,1)S(1)}, u32[]{:S(2)}) copy-start(bf16[1024,32]{1,0:T(8,128)(2,1)S(1)} %reshape_reshape_squeeze.7) | copy-start | bytes 196612
  188.4 209.8 %all-gather.30.cloned.1.call-start = ((), (), s32[]{:S(2)}) async-start(), calls=%async_computation.19 | async-start | bytes 2641920 | tf_op jit(solution)/shard_map/all_gather | solution.py:101
  274.2 40.7 %copy-start.306 = (f32[1,2,4,128]{3,1,2,0:T(2,128)S(1)}, f32[1,2,4,128]{3,1,2,0:T(2,128)}, u32[]{:S(2)}) copy-start(f32[1,2,4,128]{3,1,2,0:T(2,128)} %copy.968) | copy-start | bytes 12292
  280.2 40.0 %copy-start.390 = (f32[512]{0:T(512)}, f32[512]{0:T(512)S(1)}, u32[]{:S(2)}) copy-start(f32[512]{0:T(512)S(1)} %get-tuple-element.471) | copy-start | bytes 6148
  280.3 43.5 %copy-start.77 = (bf16[512,1024]{1,0:T(8,128)(2,1)}, bf16[512,1024]{1,0:T(8,128)(2,1)S(1)}, u32[]{:S(2)}) copy-start(bf16[512,1024]{1,0:T(8,128)(2,1)S(1)} %get-tuple-element.472) | copy-start | bytes 3145732
  280.3 43.5 %copy-start.364 = (f32[512]{0:T(512)}, f32[512]{0:T(512)S(1)}, u32[]{:S(2)}) copy-start(f32[512]{0:T(512)S(1)} %fusion.319) | copy-start | bytes 6148
  320.3 13.5 collective-permute-start.4
  352.7 82.9 %all-gather.24.cloned.1.call-start = ((), (), s32[]{:S(2)}) async-start(), calls=%async_computation.10 | async-start | bytes 4718592 | tf_op jit(solution)/shard_map/all_gather | solution.py:438
  353.5 120.7 %all-gather.26.cloned.1.call-start = ((), (), s32[]{:S(2)}) async-start(), calls=%async_computation.11 | async-start | bytes 4718592 | tf_op jit(solution)/shard_map/all_gather | solution.py:438
  355.0 126.5 %copy-start.290 = (f32[1,4,4,128]{3,1,2,0:T(4,128)}, f32[1,4,4,128]{3,1,2,0:T(4,128)S(1)}, u32[]{:S(2)}) copy-start(f32[1,4,4,128]{3,1,2,0:T(4,128)S(1)} %copy.969) | copy-start | bytes 24580
  355.1 232.6 %all-gather.32.cloned.1.call-start = ((), (), s32[]{:S(2)}) async-start(), calls=%async_computation.20 | async-start | bytes 2621440 | tf_op jit(solution)/shard_map/all_gather | solution.py:315
  372.6 140.4 %copy-start.266 = (f32[128,128]{1,0:T(8,128)}, f32[128,128]{1,0:T(8,128)S(1)}, u32[]{:S(2)}) copy-start(f32[128,128]{1,0:T(8,128)S(1)} %fusion.240) | copy-start | bytes 196612
  378.4 141.7 %copy-start.268 = (f32[128,128]{1,0:T(8,128)}, f32[128,128]{1,0:T(8,128)S(1)}, u32[]{:S(2)}) copy-start(f32[128,128]{1,0:T(8,128)S(1)} %fusion.249) | copy-start | bytes 196612
  446.1 35.5 %copy-start.382 = (f32[512]{0:T(512)}, f32[512]{0:T(512)S(1)}, u32[]{:S(2)}) copy-start(f32[512]{0:T(512)S(1)} %fusion.320) | copy-start | bytes 6148
  531.9 273.7 %all-gather.34.cloned.1.call-start = ((), (), s32[]{:S(2)}) async-start(), calls=%async_computation.21 | async-start | bytes 2621440 | tf_op jit(solution)/shard_map/all_gather | solution.py:315
  678.8 5.9 collective-permute-start.6
  717.5 207.9 %reduce-scatter.15.cloned.1.call-start = ((), (), s32[]{:S(2)}) async-start(), calls=%async_computation.16 | async-start | bytes 4718592 | tf_op jit(solution)/shard_map/reduce_scatter | solution.py:462
  723.9 201.5 %reduce-scatter.17.cloned.1.call-start = ((), (), s32[]{:S(2)}) async-start(), calls=%async_computation.17 | async-start | bytes 4718592 | tf_op jit(solution)/shard_map/reduce_scatter | solution.py:462
  732.8 195.9 %reduce-scatter.13.cloned.1.call-start = ((), (), s32[]{:S(2)}) async-start(), calls=%async_computation.15 | async-start | bytes 5308416 | tf_op jit(solution)/shard_map/reduce_scatter | solution.py:462
  805.5 257.3 %all-reduce.69.cloned.1.call-start = ((), (), s32[]{:S(2)}) async-start(), calls=%async_computation.23 | async-start | bytes 759808 | tf_op jit(solution)/shard_map/psum | solution.py:469
  888.7 10.1 collective-permute-start.7
  910.8 206.4 %reduce-scatter.9.cloned.1.call-start = ((), (), s32[]{:S(2)}) async-start(), calls=%async_computation.13 | async-start | bytes 4718592 | tf_op jit(solution)/shard_map/reduce_scatter | solution.py:462
  916.6 255.5 %reduce-scatter.11.cloned.1.call-start = ((), (), s32[]{:S(2)}) async-start(), calls=%async_computation.14 | async-start | bytes 4718592 | tf_op jit(solution)/shard_map/reduce_scatter | solution.py:462
  925.3 321.3 %all-reduce.73.cloned.1.call-start = ((), (), s32[]{:S(2)}) async-start(), calls=%async_computation.25 | async-start | bytes 3276800 | tf_op jit(solution)/shard_map/psum | solution.py:546
  928.8 374.5 %reduce-scatter.7.cloned.1.call-start = ((), (), s32[]{:S(2)}) async-start(), calls=%async_computation.12 | async-start | bytes 5308416 | tf_op jit(solution)/shard_map/reduce_scatter | solution.py:462
  937.0 7.2 collective-permute-start.5
  944.2 433.6 %all-reduce.71.cloned.1.call-start = ((), (), s32[]{:S(2)}) async-start(), calls=%async_computation.24 | async-start | bytes 3276800 | tf_op jit(solution)/shard_map/psum | solution.py:546
  951.4 357.8 %collective-permute-start.8 = (bf16[1,512,1024]{2,1,0:T(8,128)(2,1)}, bf16[1,512,1024]{2,1,0:T(8,128)(2,1)}, u32[]{:S(2)}, u32[]{:S(2)}) collective-permute-start(bf16[1,512,1024]{2,1,0:T(8,128)(2,1)} %fusion.127), channel_id=1, source_target_pairs={{0,16},{16,0},{1,17},{17,1},{2,18},{18,2},{3,19},{19,3},{4,20},{20... | collective-permute-start | bytes 3145736 | tf_op jit(solution)/shard_map/ppermute | solution.py:573
  1309.1 68.7 %copy-start.124 = (bf16[128,2048]{1,0:T(8,128)(2,1)S(1)}, bf16[128,2048]{1,0:T(8,128)(2,1)}, u32[]{:S(2)}) copy-start(bf16[128,2048]{1,0:T(8,128)(2,1)} %get-tuple-element.28) | copy-start | bytes 1572868
  1378.0 6.2 collective-permute-start.9
  1383.3 2.1 collective-permute-start.11
  1384.1 4.7 collective-permute-start.10
  (409 other events, 2229.0 us)
Sparse Core Ops, SparseCore 0:
  18.2 55.5 all-reduce.66
  76.3 38.3 all-gather.15
  153.7 44.7 all-gather.27
  200.3 35.4 all-gather.17
  237.5 36.7 all-gather.19
  276.0 38.9 all-gather.21
  352.8 45.3 all-gather.29
  400.1 35.4 all-gather.23
  437.5 36.7 all-gather.25
  532.0 45.9 all-gather.31
  717.6 45.6 all-gather.33
  766.5 49.8 reduce-scatter.14
  820.1 51.3 reduce-scatter.16
  874.8 53.9 reduce-scatter.12
  935.5 127.3 all-reduce.68
  1066.1 51.0 reduce-scatter.8
  1120.8 51.2 reduce-scatter.10
  1174.5 71.9 all-reduce.72
  1250.4 52.8 reduce-scatter.6
  1305.8 72.0 all-reduce.70

commit v2 on v1

--- a/solution.py
+++ b/solution.py
@@ -286,6 +286,21 @@
     grad_inner, grad_outer, grad_values_skip, skip_gain_grad, grad_gate_pre, output_gain_grad = (
         exit_back(grad_normed_out)
     )
+    grad_gate_low = grad_gate_pre.astype(jnp.bfloat16)
+    gate_proj_grad = jnp.einsum(
+        "td,te->de", normed_low, grad_gate_low, preferred_element_type=jnp.float32
+    )
+    grad_inner, grad_outer, grad_values_skip, out_proj_grad, gate_proj_grad = (
+        lax.optimization_barrier(
+            (
+                grad_inner,
+                grad_outer,
+                grad_values_skip,
+                out_proj_grad.astype(jnp.bfloat16),
+                gate_proj_grad.astype(jnp.bfloat16),
+            )
+        )
+    )
     grad_inner_low = grad_inner.astype(jnp.bfloat16)
     grad_mixings = []
     grad_values_inner = []
@@ -359,15 +374,11 @@
     )
     back_rim = passed_along(grad_extended[:rim_rows], "seq", -1)
     grad_mixed = grad_extended[rim_rows:] + jnp.pad(back_rim, ((length - rim_rows, 0), (0, 0)))
-    grad_gate_low = grad_gate_pre.astype(jnp.bfloat16)
     grad_mixed_low = grad_mixed.astype(jnp.bfloat16)
     grad_step_low = grad_step_raw.astype(jnp.bfloat16)
-    gate_proj_grad = jnp.einsum(
-        "td,te->de", normed_low, grad_gate_low, preferred_element_type=jnp.float32
-    )
     mixed_proj_grad = jnp.einsum(
         "td,te->de", normed_low, grad_mixed_low, preferred_element_type=jnp.float32
-    )
+    ).astype(jnp.bfloat16)
     step_proj_grad = jnp.einsum(
         "td,te->de", normed_low, grad_step_low, preferred_element_type=jnp.float32
     )
@@ -403,10 +414,11 @@
 
 def fetch_small(shards):
     flat = jnp.concatenate([shards[at].reshape(-1) for at, _ in SMALL])
-    gathered = lax.all_gather(flat, ("section", "wa"))
+    flat = jnp.pad(flat, (0, -flat.shape[0] % 2048)).reshape(-1, 128)
+    gathered = lax.all_gather(flat, ("wa", "section"), axis=0, tiled=True)
     sections = lax.axis_size("section")
     count = lax.axis_size("wa")
-    gathered = gathered.reshape(sections, count, -1)
+    gathered = jnp.moveaxis(gathered.reshape(count, sections, -1), 1, 0)
     layers = []
     for level in range(sections):
         whole = {}
@@ -459,14 +471,18 @@
 
 
 def scatter_large(grad):
-    return lax.psum_scatter(
-        grad.astype(jnp.bfloat16), ("wa", "section"), scatter_dimension=0, tiled=True
-    )
-
-
-def reduce_small(grads):
-    flat = jnp.concatenate([grads[at].reshape(-1) for at, _ in SMALL])
-    return lax.psum(flat, ("section", "wa", "seq"))
+    sections = lax.axis_size("section")
+    rank = lax.axis_index("section")
+    count = lax.axis_size("wa")
+    rows, columns = grad.shape
+    cut = grad.reshape(count, sections, rows // (count * sections), columns)
+    total = lax.dynamic_index_in_dim(cut, rank, 1, False).astype(jnp.float32)
+    for hop in range(1, sections):
+        block = lax.dynamic_index_in_dim(cut, lax.rem(rank + hop, sections), 1, False)
+        came = lax.ppermute(block, "section", [(i, (i + hop) % sections) for i in range(sections)])
+        total = total + came.astype(jnp.float32)
+    total = total.astype(jnp.bfloat16).reshape(rows // sections, columns)
+    return lax.psum_scatter(total, "wa", scatter_dimension=0, tiled=True)
 
 
 def on_device(
@@ -525,28 +541,38 @@
         grad = lax.dynamic_index_in_dim(cotangent[:, 0], own, 0, False).astype(jnp.float32)
         for level in reversed(range(sections)):
             grad, grads = layer_back(grad, params[level], tapes[level])
+            grad, grads = lax.optimization_barrier((grad, grads))
             backs[level][turn] = grad
             if totals[level] is None:
                 totals[level] = grads
             else:
-                totals[level] = tuple(a + b for a, b in zip(totals[level], grads))
+                totals[level] = tuple(
+                    (a.astype(jnp.float32) + b.astype(jnp.float32)).astype(a.dtype)
+                    for a, b in zip(totals[level], grads)
+                )
 
     layer_out = gather_micro(outs, rank, sections, share)[None, :, None]
     input_grad = gather_micro(backs, rank, sections, share)[None, :, None]
 
     final = {}
-    parts = [None] * sections
+    parts = [dict() for _ in range(sections)]
     sums = [None] * sections
     before = None
+    sum_before = None
     for level in reversed(range(sections)):
-        scattered = tuple(scatter_large(totals[level][at]) for at in LARGE)
-        if before is not None:
-            scattered, before = lax.optimization_barrier((scattered, before))
-            parts[level + 1] = before
-        before = lax.psum(scattered, "seq")
-        parts[level] = before
-        sums[level] = reduce_small(totals[level])
-    parts = [dict(zip(LARGE, part)) for part in parts]
+        for at in (10, 1, 2):
+            scattered = scatter_large(totals[level][at])
+            if before is not None:
+                scattered, parts[before[0]][before[1]] = lax.optimization_barrier(
+                    (scattered, parts[before[0]][before[1]])
+                )
+            parts[level][at] = lax.psum(scattered, "seq")
+            before = (level, at)
+        flat = jnp.concatenate([totals[level][at].reshape(-1) for at, _ in SMALL])
+        if sum_before is not None:
+            flat, sums[sum_before] = lax.optimization_barrier((flat, sums[sum_before]))
+        sums[level] = lax.psum(flat, ("section", "wa", "seq"))
+        sum_before = level
     for at in LARGE:
         stacked = jnp.stack([parts[level][at] for level in range(sections)])
         got = swapped(stacked, rank, sections)

time: 1410 us -> 1510 us (1.071)
  waiting for transfers between devices: 620 us -> 659 us
  local copies, waits for them, and re-layouts: 228 us -> 254 us
    psum x3 -> x8, waiting for transfers between devices: 248 us -> 416 us  [the longest x2 246 us: on_device(): sums[level] = lax.psum(flat, ('section', 'wa', 'seq'))]
    reduce_scatter x6, waiting for transfers between devices: 168 us -> 106 us  [scatter_large(): return lax.psum_scatter(total, 'wa', scatter_dimension=0, tiled=True)]
    unnamed x21 -> x24, waiting for transfers between devices: 53.6 us -> 1.07 us
    convert_element_type x1 -> x9, other arithmetic: 0.66 us -> 27.4 us  [the longest x6 25.4 us: scatter_large(): total = total.astype(jnp.bfloat16).reshape(rows // sections, columns)]
    squeeze x0 -> x6, local copies, waits for them, and re-layouts: none -> 16.2 us  [scatter_large(): lax.dynamic_index_in_dim(cut, lax.rem(rank + hop, sections), 1, False)]
    unnamed x896 -> x915, local copies, waits for them, and re-layouts: 41 us -> 38.7 us
  transfers between devices with their start and end apart: 32 -> 42, of which waited for: 18 -> 22; matrix products, arithmetic and copies ran while one was open for 36% -> 35% of each run, Pallas kernels for 0% -> 0%
where the time goes in v2:
time: 1510 us; the launch traced here: 1500 us
  waiting for transfers between devices  659 us (44%)
  matrix products  283 us (19%)
  local copies, waits for them, and re-layouts  254 us (17%)
  other arithmetic  253 us (17%)
  between operations  20 us (1%)
  starting transfers between devices  15.3 us (1%)
    psum x2, waiting for transfers between devices, on_device(): sums[level] = lax.psum(flat, ('section', 'wa', 'seq'))  246 us
    psum x6, waiting for transfers between devices, on_device(): parts[level][at] = lax.psum(scattered, 'seq')  170 us
    all_gather x6, waiting for transfers between devices, fetch_large(): lax.all_gather(pieces[level], ('wa', 'section'), axis=0, tiled=True)  116 us
    reduce_scatter x6, waiting for transfers between devices, scatter_large(): return lax.psum_scatter(total, 'wa', scatter_dimension=0, tiled=True)  106 us
    unnamed x915, local copies, waits for them, and re-layouts  38.7 us
    dot_general x24, matrix products, block_piece(): fresh_state = jnp.einsum('sd,sn->dn', scaled, keys_in, precision=HIGHEST)  37.7 us
    dot_general x24, matrix products, reach_piece(): reach_mat = jnp.einsum('tn,dn->td', queries, start_state, precision=HIGHEST)  36.4 us
    dot_general x8, matrix products, layer_back(): jnp.einsum('thp,shp->hts', grad_heads, heads_view, preferred_element_type...  30.4 us
  transfers between devices with their start and end apart: 42, of which 22 were waited for; matrix products, arithmetic and copies ran while one was open for 35% of the time, Pallas kernels for 0%

profile of v2, /device:TPU:0, one launch (start us, length us, event | category | flops | bytes accessed | tf_op | source)
XLA Modules:
  0.0 1495.5 jit_solution(5820318338044747252)
XLA Ops:
  13.4 10.6 all_gather.41
  33.0 21.4 %all-gather.15.cloned.1.call-done = bf16[1024,2304]{1,0:T(8,128)(2,1)} async-done(((bf16[128,2304]{1,0:T(8,128)(2,1)}), bf16[1024,2304]{1,0:T(8,128)(2,1)}) %all-gather.15.cloned.1.call-update) | async-done | bytes 4718608 | tf_op jit(solution)/shard_map/all_gather | solution.py:450
  54.5 5.3 convolution_convert_fusion.3
  61.9 4.0 collective-permute-start.1
  79.5 4.5 fusion.405
  162.2 4.0 fusion.89
  177.8 12.4 multiply_reduce_fusion.19
  190.2 24.1 %all-gather.19.cloned.1.call-done = bf16[2048,1024]{1,0:T(8,128)(2,1)} async-done(((bf16[256,1024]{1,0:T(8,128)(2,1)}), bf16[2048,1024]{1,0:T(8,128)(2,1)}) %all-gather.19.cloned.1.call-update) | async-done | bytes 4194320 | tf_op jit(solution)/shard_map/all_gather | solution.py:450
  214.4 6.2 fusion.44
  225.5 29.6 %all-gather.21.cloned.1.call-done = bf16[1024,2304]{1,0:T(8,128)(2,1)} async-done(((bf16[128,2304]{1,0:T(8,128)(2,1)}), bf16[1024,2304]{1,0:T(8,128)(2,1)}) %all-gather.21.cloned.1.call-update) | async-done | bytes 4718608 | tf_op jit(solution)/shard_map/all_gather | solution.py:450
  255.1 5.3 convolution_convert_fusion.2
  275.8 4.6 fusion.400
  287.3 5.7 concatenate.132
  332.8 5.5 all-gather.29.cloned.1.call-done
  340.5 3.4 fusion.102
  343.9 3.6 maximum_add_fusion.3
  357.4 18.5 %all-gather.23.cloned.1.call-done = bf16[1024,2048]{1,0:T(8,128)(2,1)} async-done(((bf16[128,2048]{1,0:T(8,128)(2,1)}), bf16[1024,2048]{1,0:T(8,128)(2,1)}) %all-gather.23.cloned.1.call-update) | async-done | bytes 4194320 | tf_op jit(solution)/shard_map/all_gather | solution.py:450
  376.0 10.0 multiply_reduce_fusion.18
  387.9 4.5 convolution_convert_fusion.7
  392.5 22.1 %all-gather.25.cloned.1.call-done = bf16[2048,1024]{1,0:T(8,128)(2,1)} async-done(((bf16[256,1024]{1,0:T(8,128)(2,1)}), bf16[2048,1024]{1,0:T(8,128)(2,1)}) %all-gather.25.cloned.1.call-update) | async-done | bytes 4194320 | tf_op jit(solution)/shard_map/all_gather | solution.py:450
  414.6 7.3 multiply_reduce_fusion.13
  422.0 6.2 multiply_reduce_fusion.14
  430.9 4.5 convolution_convert_fusion.6
  470.0 3.5 slice_multiply_fusion.30
  477.9 5.7 multiply_reduce_fusion.15
  524.4 10.2 fusion.71
  541.2 4.8 multiply_reduce_fusion.42
  589.1 8.9 slice_multiply_fusion.6
  623.9 11.4 multiply_reduce_fusion.7
  635.4 7.4 broadcast_multiply_fusion
  657.1 3.6 fusion.34
  661.3 4.9 convolution_convert_fusion.1
  668.3 8.9 multiply_reduce_fusion.8
  677.2 3.9 fusion.16
  681.2 11.9 multiply_reduce_fusion.9
  701.0 4.4 convolution_convert_fusion.4
  705.5 4.5 convolution_convert_fusion.5
  717.9 3.5 multiply_reduce_fusion.10
  721.9 6.0 slice_multiply_fusion.22
  753.8 3.7 fusion.17
  783.5 8.1 fusion.79
  798.3 4.5 fusion.6
  804.0 5.3 multiply_reduce_fusion.38
  830.2 5.7 slice_multiply_fusion.14
  838.7 11.1 multiply_reduce_fusion.3
  849.8 7.5 broadcast_multiply_fusion.4
  881.1 4.0 collective-permute-done.7
  885.1 6.8 fusion.221
  896.7 4.7 convolution_convert_fusion
  904.3 36.2 %all-reduce.74.cloned.1.call-done = bf16[128,2048]{1,0:T(8,128)(2,1)} async-done(((bf16[128,2048]{1,0:T(8,128)(2,1)}), bf16[128,2048]{1,0:T(8,128)(2,1)}) %all-reduce.74.cloned.1.call-update) | async-done | bytes 524304 | tf_op jit(solution)/shard_map/psum | solution.py:569
  940.6 4.5 fusion.18
  948.9 120.6 %all-reduce.68.cloned.1.call-done = f32[47456]{0:T(1024)} async-done(((f32[47456]{0:T(1024)}), f32[47456]{0:T(1024)}) %all-reduce.68.cloned.1.call-update) | async-done | bytes 189840 | tf_op jit(solution)/shard_map/psum | solution.py:574
  1070.4 4.5 fusion.19
  1078.5 5.8 fusion.69
  1096.5 15.3 %all-reduce.76.cloned.1.call-done = bf16[128,2304]{1,0:T(8,128)(2,1)} async-done(((bf16[128,2304]{1,0:T(8,128)(2,1)}), bf16[128,2304]{1,0:T(8,128)(2,1)}) %all-reduce.76.cloned.1.call-update) | async-done | bytes 589840 | tf_op jit(solution)/shard_map/psum | solution.py:569
  1111.8 38.3 %reduce-scatter.11.cloned.1.call-done = bf16[256,1024]{1,0:T(8,128)(2,1)} async-done(((bf16[1024,1024]{1,0:T(8,128)(2,1)}), bf16[256,1024]{1,0:T(8,128)(2,1)}) %reduce-scatter.11.cloned.1.call-update) | async-done | bytes 524304 | tf_op jit(solution)/shard_map/reduce_scatter | solution.py:485
  1150.2 4.3 fusion.7
  1154.6 125.0 %all-reduce.70.cloned.1.call-done = f32[1,47456]{1,0:T(1,128)} async-done(((f32[1,47456]{1,0:T(1,128)}), f32[1,47456]{1,0:T(1,128)}) %all-reduce.70.cloned.1.call-update) | async-done | bytes 189840 | tf_op jit(solution)/shard_map/psum | solution.py:574
  1286.8 32.6 %reduce-scatter.9.cloned.1.call-done = bf16[128,2048]{1,0:T(8,128)(2,1)} async-done(((bf16[512,2048]{1,0:T(8,128)(2,1)}), bf16[128,2048]{1,0:T(8,128)(2,1)}) %reduce-scatter.9.cloned.1.call-update) | async-done | bytes 524304 | tf_op jit(solution)/shard_map/reduce_scatter | solution.py:485
  1319.4 40.6 %all-reduce.78.cloned.1.call-done = bf16[256,1024]{1,0:T(8,128)(2,1)} async-done(((bf16[256,1024]{1,0:T(8,128)(2,1)}), bf16[256,1024]{1,0:T(8,128)(2,1)}) %all-reduce.78.cloned.1.call-update) | async-done | bytes 524304 | tf_op jit(solution)/shard_map/psum | solution.py:569
  1360.4 3.4 convert_select_fusion.1
  1366.1 34.9 %reduce-scatter.7.cloned.1.call-done = bf16[128,2304]{1,0:T(8,128)(2,1)} async-done(((bf16[512,2304]{1,0:T(8,128)(2,1)}), bf16[128,2304]{1,0:T(8,128)(2,1)}) %reduce-scatter.7.cloned.1.call-update) | async-done | bytes 589840 | tf_op jit(solution)/shard_map/reduce_scatter | solution.py:485
  1401.1 40.7 %all-reduce.80.cloned.1.call-done = bf16[128,2048]{1,0:T(8,128)(2,1)} async-done(((bf16[128,2048]{1,0:T(8,128)(2,1)}), bf16[128,2048]{1,0:T(8,128)(2,1)}) %all-reduce.80.cloned.1.call-update) | async-done | bytes 524304 | tf_op jit(solution)/shard_map/psum | solution.py:569
  1445.7 37.4 %all-reduce.82.cloned.1.call-done = bf16[1,128,2304]{2,1,0:T(8,128)(2,1)} async-done(((bf16[1,128,2304]{2,1,0:T(8,128)(2,1)}), bf16[1,128,2304]{2,1,0:T(8,128)(2,1)}) %all-reduce.82.cloned.1.call-update) | async-done | bytes 589840 | tf_op jit(solution)/shard_map/psum | solution.py:569
  (1576 shorter events, 542.9 us)
Async XLA Ops:
  7.3 47.2 %all-gather.15.cloned.1.call-start = ((), (), s32[]{:S(2)}) async-start(), calls=%async_computation.6 | async-start | bytes 5308416 | tf_op jit(solution)/shard_map/all_gather | solution.py:450
  8.4 2.1 collective-permute-start
  12.8 147.3 %all-gather.27.cloned.1.call-start = ((), (), s32[]{:S(2)}) async-start(), calls=%async_computation.26 | async-start | bytes 2641920 | tf_op jit(solution)/shard_map/all_gather | solution.py:101
  32.3 77.7 %copy-start.185 = (f32[1,32]{0,1:T(8,128)}, f32[1,32]{0,1:T(8,128)S(1)}, u32[]{:S(2)}) copy-start(f32[1,32]{0,1:T(8,128)S(1)} %get-tuple-element.341) | copy-start | bytes 388
  61.9 15.3 %collective-permute-start.1 = (bf16[3,2304]{1,0:T(4,128)(2,1)}, bf16[3,2304]{1,0:T(4,128)(2,1)}, u32[]{:S(2)}, u32[]{:S(2)}) collective-permute-start(bf16[3,2304]{1,0:T(4,128)(2,1)} %slice.908), channel_id=1, source_target_pairs={{0,4},{4,8},{8,12},{1,5},{5,9},{9,13},{2,6},{6,10},{10,14},{3,7},{... | collective-permute-start | bytes 41480 | tf_op jit(solution)/shard_map/ppermute | solution.py:17
  86.0 80.3 %copy-start.21 = (f32[2048,128]{1,0:T(8,128)}, f32[2048,128]{1,0:T(8,128)S(1)}, u32[]{:S(2)}) copy-start(f32[2048,128]{1,0:T(8,128)S(1)} %convolution_add_fusion.7) | copy-start | bytes 3145732
  93.6 84.2 %all-gather.17.cloned.1.call-start = ((), (), s32[]{:S(2)}) async-start(), calls=%async_computation.7 | async-start | bytes 4718592 | tf_op jit(solution)/shard_map/all_gather | solution.py:450
  94.9 2.0 collective-permute-start.2
  98.1 116.3 %all-gather.19.cloned.1.call-start = ((), (), s32[]{:S(2)}) async-start(), calls=%async_computation.8 | async-start | bytes 4718592 | tf_op jit(solution)/shard_map/all_gather | solution.py:450
  98.2 2.0 collective-permute-start.3
  101.3 153.9 %all-gather.21.cloned.1.call-start = ((), (), s32[]{:S(2)}) async-start(), calls=%async_computation.9 | async-start | bytes 5308416 | tf_op jit(solution)/shard_map/all_gather | solution.py:450
  109.9 44.5 %copy-start.328 = (f32[32,128]{1,0:T(8,128)}, f32[32,128]{1,0:T(8,128)S(1)}, u32[]{:S(2)}) copy-start(f32[32,128]{1,0:T(8,128)S(1)} %copy.757) | copy-start | bytes 49156
  110.4 55.8 %copy-start.169 = (f32[4,2048]{1,0:T(4,128)}, f32[4,2048]{1,0:T(4,128)S(1)}, u32[]{:S(2)}) copy-start(f32[4,2048]{1,0:T(4,128)S(1)} %mul.1716) | copy-start | bytes 98308
  110.9 61.9 %copy-start.24 = (f32[128,2048]{1,0:T(8,128)}, f32[128,2048]{1,0:T(8,128)S(1)}, u32[]{:S(2)}) copy-start(f32[128,2048]{1,0:T(8,128)S(1)} %copy.793) | copy-start | bytes 3145732
  114.2 60.9 %copy-start.26 = (f32[128,2048]{1,0:T(8,128)}, f32[128,2048]{1,0:T(8,128)S(1)}, u32[]{:S(2)}) copy-start(f32[128,2048]{1,0:T(8,128)S(1)} %copy.791) | copy-start | bytes 3145732
  121.6 39.9 %copy-start.413 = (pred[4]{0:T(512)(128)(4,1)}, pred[4]{0:T(512)(128)(4,1)S(1)}, u32[]{:S(2)}) copy-start(pred[4]{0:T(512)(128)(4,1)S(1)} %get-tuple-element.561) | copy-start | bytes 16
  122.2 38.7 %copy-start.409 = (pred[4,4]{1,0:T(4,128)(4,1)}, pred[4,4]{1,0:T(4,128)(4,1)S(1)}, u32[]{:S(2)}) copy-start(pred[4,4]{1,0:T(4,128)(4,1)S(1)} %fusion.334) | copy-start | bytes 52
  122.2 38.6 %copy-start.411 = (pred[4,4]{1,0:T(4,128)(4,1)}, pred[4,4]{1,0:T(4,128)(4,1)S(1)}, u32[]{:S(2)}) copy-start(pred[4,4]{1,0:T(4,128)(4,1)S(1)} %fusion.333) | copy-start | bytes 52
  122.9 91.5 %copy-start.293 = (f32[1,4,512]{2,0,1:T(1,128)}, f32[1,4,512]{2,0,1:T(1,128)S(1)}, u32[]{:S(2)}) copy-start(f32[1,4,512]{2,0,1:T(1,128)S(1)} %get-tuple-element.413) | copy-start | bytes 24580
  122.9 215.5 %all-gather.29.cloned.1.call-start = ((), (), s32[]{:S(2)}) async-start(), calls=%async_computation.27 | async-start | bytes 2641920 | tf_op jit(solution)/shard_map/all_gather | solution.py:101
  220.6 39.8 %copy-start.78 = (bf16[512,1024]{1,0:T(8,128)(2,1)}, bf16[512,1024]{1,0:T(8,128)(2,1)S(1)}, u32[]{:S(2)}) copy-start(bf16[512,1024]{1,0:T(8,128)(2,1)S(1)} %get-tuple-element.544) | copy-start | bytes 3145732
  220.6 39.8 %copy-start.369 = (f32[512]{0:T(512)}, f32[512]{0:T(512)S(1)}, u32[]{:S(2)}) copy-start(f32[512]{0:T(512)S(1)} %fusion.337) | copy-start | bytes 6148
  222.3 38.1 %copy-start.176 = (f32[512,32]{0,1:T(8,128)}, f32[512,32]{0,1:T(8,128)S(1)}, u32[]{:S(2)}) copy-start(f32[512,32]{0,1:T(8,128)S(1)} %get-tuple-element.445) | copy-start | bytes 196612
  222.9 37.5 %copy-start.164 = (f32[128,32]{1,0:T(8,128)}, f32[128,32]{1,0:T(8,128)S(1)}, u32[]{:S(2)}) copy-start(f32[128,32]{1,0:T(8,128)S(1)} %reduce_window_sum.84) | copy-start | bytes 49156
  223.3 37.2 %copy-start.165 = (f32[128,32]{1,0:T(8,128)}, f32[128,32]{1,0:T(8,128)S(1)}, u32[]{:S(2)}) copy-start(f32[128,32]{1,0:T(8,128)S(1)} %reduce_window_sum.83) | copy-start | bytes 49156
  225.5 39.9 %copy-start.418 = (bf16[64]{0:T(256)(128)(2,1)S(1)}, bf16[64]{0:T(256)(128)(2,1)}, u32[]{:S(2)}) copy-start(bf16[64]{0:T(256)(128)(2,1)} %copy-done.417) | copy-start | bytes 388
  262.0 11.6 collective-permute-start.4
  293.1 82.8 %all-gather.23.cloned.1.call-start = ((), (), s32[]{:S(2)}) async-start(), calls=%async_computation.10 | async-start | bytes 4718592 | tf_op jit(solution)/shard_map/all_gather | solution.py:450
  293.8 120.7 %all-gather.25.cloned.1.call-start = ((), (), s32[]{:S(2)}) async-start(), calls=%async_computation.11 | async-start | bytes 4718592 | tf_op jit(solution)/shard_map/all_gather | solution.py:450
  295.4 245.8 %all-gather.31.cloned.1.call-start = ((), (), s32[]{:S(2)}) async-start(), calls=%async_computation.28 | async-start | bytes 2621440 | tf_op jit(solution)/shard_map/all_gather | solution.py:330
  483.6 314.6 %reduce-scatter.17.cloned.1.call-start = ((), (), s32[]{:S(2)}) async-start(), calls=%async_computation.19 | async-start | bytes 2621440 | tf_op jit(solution)/shard_map/reduce_scatter | solution.py:485
  648.4 5.9 collective-permute-start.6
  661.3 44.2 %copy-start.14 = (f32[512,1024]{1,0:T(8,128)}, f32[512,1024]{1,0:T(8,128)S(1)}, u32[]{:S(2)}) copy-start(f32[512,1024]{1,0:T(8,128)S(1)} %fusion.42) | copy-start | bytes 6291460
  667.6 9.5 collective-permute-start.14
  681.1 121.9 %all-gather.33.cloned.1.call-start = ((), (), s32[]{:S(2)}) async-start(), calls=%async_computation.29 | async-start | bytes 2621440 | tf_op jit(solution)/shard_map/all_gather | solution.py:330
  697.1 56.7 %collective-permute-start.13 = (bf16[4,128,2048]{2,1,0:T(8,128)(2,1)}, bf16[4,128,2048]{2,1,0:T(8,128)(2,1)}, u32[]{:S(2)}, u32[]{:S(2)}) collective-permute-start(bf16[4,128,2048]{2,1,0:T(8,128)(2,1)} %dynamic-slice_bitcast_fusion.3), channel_id=1, source_target_pairs={{0,16},{16,0},{1,17},{17,1},{2,18},{18,2},{3,19},{19,3},{4,20},{20... | collective-permute-start | bytes 6291464 | tf_op jit(solution)/shard_map/ppermute | solution.py:482
  700.9 97.4 %collective-permute-start.12 = (bf16[4,128,2304]{2,1,0:T(8,128)(2,1)}, bf16[4,128,2304]{2,1,0:T(8,128)(2,1)}, u32[]{:S(2)}, u32[]{:S(2)}) collective-permute-start(bf16[4,128,2304]{2,1,0:T(8,128)(2,1)} %dynamic-slice_bitcast_fusion), channel_id=1, source_target_pairs={{0,16},{16,0},{1,17},{17,1},{2,18},{18,2},{3,19},{19,3},{4,20},{20... | collective-permute-start | bytes 7077896 | tf_op jit(solution)/shard_map/ppermute | solution.py:482
  721.4 181.5 %reduce-scatter.15.cloned.1.call-start = ((), (), s32[]{:S(2)}) async-start(), calls=%async_computation.18 | async-start | bytes 2621440 | tf_op jit(solution)/shard_map/reduce_scatter | solution.py:485
  757.5 145.4 %all-reduce.72.cloned.1.call-start = ((), (), s32[]{:S(2)}) async-start(), calls=%async_computation.20 | async-start | bytes 1048576 | tf_op jit(solution)/shard_map/psum | solution.py:569
  798.2 106.1 %reduce-scatter.13.cloned.1.call-start = ((), (), s32[]{:S(2)}) async-start(), calls=%async_computation.17 | async-start | bytes 2949120 | tf_op jit(solution)/shard_map/reduce_scatter | solution.py:485
  802.8 137.7 %all-reduce.74.cloned.1.call-start = ((), (), s32[]{:S(2)}) async-start(), calls=%async_computation.21 | async-start | bytes 1048576 | tf_op jit(solution)/shard_map/psum | solution.py:569
  879.2 5.9 collective-permute-start.7
  902.9 37.7 %collective-permute-start.11 = (bf16[4,256,1024]{2,1,0:T(8,128)(2,1)}, bf16[4,256,1024]{2,1,0:T(8,128)(2,1)}, u32[]{:S(2)}, u32[]{:S(2)}) collective-permute-start(bf16[4,256,1024]{2,1,0:T(8,128)(2,1)} %dynamic-slice_bitcast_fusion.4), channel_id=1, source_target_pairs={{0,16},{16,0},{1,17},{17,1},{2,18},{18,2},{3,19},{19,3},{4,20},{20... | collective-permute-start | bytes 6291464 | tf_op jit(solution)/shard_map/ppermute | solution.py:482
  902.9 166.6 %all-reduce.68.cloned.1.call-start = ((), (), s32[]{:S(2)}) async-start(), calls=%async_computation.12 | async-start | bytes 385024 | tf_op jit(solution)/shard_map/psum | solution.py:574
  904.2 207.5 %all-reduce.76.cloned.1.call-start = ((), (), s32[]{:S(2)}) async-start(), calls=%async_computation.22 | async-start | bytes 1179648 | tf_op jit(solution)/shard_map/psum | solution.py:569
  940.6 209.5 %reduce-scatter.11.cloned.1.call-start = ((), (), s32[]{:S(2)}) async-start(), calls=%async_computation.16 | async-start | bytes 2621440 | tf_op jit(solution)/shard_map/reduce_scatter | solution.py:485
  945.2 334.4 %all-reduce.70.cloned.1.call-start = ((), (), s32[]{:S(2)}) async-start(), calls=%async_computation.13 | async-start | bytes 379904 | tf_op jit(solution)/shard_map/psum | solution.py:574
  948.4 122.0 %collective-permute-start.10 = (bf16[4,128,2048]{2,1,0:T(8,128)(2,1)}, bf16[4,128,2048]{2,1,0:T(8,128)(2,1)}, u32[]{:S(2)}, u32[]{:S(2)}) collective-permute-start(bf16[4,128,2048]{2,1,0:T(8,128)(2,1)} %dynamic-slice_bitcast_fusion.5), channel_id=1, source_target_pairs={{0,16},{16,0},{1,17},{17,1},{2,18},{18,2},{3,19},{19,3},{4,20},{20... | collective-permute-start | bytes 6291464 | tf_op jit(solution)/shard_map/ppermute | solution.py:482
  1070.4 249.0 %reduce-scatter.9.cloned.1.call-start = ((), (), s32[]{:S(2)}) async-start(), calls=%async_computation.15 | async-start | bytes 2621440 | tf_op jit(solution)/shard_map/reduce_scatter | solution.py:485
  1074.9 285.1 %all-reduce.78.cloned.1.call-start = ((), (), s32[]{:S(2)}) async-start(), calls=%async_computation.23 | async-start | bytes 1048576 | tf_op jit(solution)/shard_map/psum | solution.py:569
  1078.5 71.7 %collective-permute-start.9 = (bf16[4,128,2304]{2,1,0:T(8,128)(2,1)}, bf16[4,128,2304]{2,1,0:T(8,128)(2,1)}, u32[]{:S(2)}, u32[]{:S(2)}) collective-permute-start(bf16[4,128,2304]{2,1,0:T(8,128)(2,1)} %dynamic-slice_bitcast_fusion.1), channel_id=1, source_target_pairs={{0,16},{16,0},{1,17},{17,1},{2,18},{18,2},{3,19},{19,3},{4,20},{20... | collective-permute-start | bytes 7077896 | tf_op jit(solution)/shard_map/ppermute | solution.py:482
  1086.7 3.1 collective-permute-start.5
  1095.5 264.9 %collective-permute-start.8 = (bf16[1,512,1024]{2,1,0:T(8,128)(2,1)}, bf16[1,512,1024]{2,1,0:T(8,128)(2,1)}, u32[]{:S(2)}, u32[]{:S(2)}) collective-permute-start(bf16[1,512,1024]{2,1,0:T(8,128)(2,1)} %fusion.132), channel_id=1, source_target_pairs={{0,16},{16,0},{1,17},{17,1},{2,18},{18,2},{3,19},{19,3},{4,20},{20... | collective-permute-start | bytes 3145736 | tf_op jit(solution)/shard_map/ppermute | solution.py:599
  1150.1 251.0 %reduce-scatter.7.cloned.1.call-start = ((), (), s32[]{:S(2)}) async-start(), calls=%async_computation.14 | async-start | bytes 2949120 | tf_op jit(solution)/shard_map/reduce_scatter | solution.py:485
  1154.5 205.5 %copy-start.135 = (bf16[256,1024]{1,0:T(8,128)(2,1)S(1)}, bf16[256,1024]{1,0:T(8,128)(2,1)}, u32[]{:S(2)}) copy-start(bf16[256,1024]{1,0:T(8,128)(2,1)} %all-reduce.72.cloned.1.call-done) | copy-start | bytes 1572868
  1154.5 287.2 %all-reduce.80.cloned.1.call-start = ((), (), s32[]{:S(2)}) async-start(), calls=%async_computation.24 | async-start | bytes 1048576 | tf_op jit(solution)/shard_map/psum | solution.py:569
  1360.2 82.5 %collective-permute-start.17 = (bf16[256,1024]{1,0:T(8,128)(2,1)S(1)}, bf16[256,1024]{1,0:T(8,128)(2,1)}, u32[]{:S(2)}, u32[]{:S(2)}) collective-permute-start(bf16[256,1024]{1,0:T(8,128)(2,1)S(1)} %fusion.203), channel_id=1, source_target_pairs={{0,16},{16,0},{1,17},{17,1},{2,18},{18,2},{3,19},{19,3},{4,20},{20... | collective-permute-start | bytes 1572872 | tf_op jit(solution)/shard_map/ppermute | solution.py:463
  1360.3 122.7 %all-reduce.82.cloned.1.call-start = ((), (), s32[]{:S(2)}) async-start(), calls=%async_computation.25 | async-start | bytes 1179648 | tf_op jit(solution)/shard_map/psum | solution.py:569
  1363.8 78.0 %copy-start.136 = (bf16[128,2048]{1,0:T(8,128)(2,1)S(1)}, bf16[128,2048]{1,0:T(8,128)(2,1)}, u32[]{:S(2)}) copy-start(bf16[128,2048]{1,0:T(8,128)(2,1)} %all-reduce.74.cloned.1.call-done) | copy-start | bytes 1572868
  1366.1 76.6 %copy-start.140 = (bf16[256,1024]{1,0:T(8,128)(2,1)S(1)}, bf16[256,1024]{1,0:T(8,128)(2,1)}, u32[]{:S(2)}) copy-start(bf16[256,1024]{1,0:T(8,128)(2,1)} %all-reduce.78.cloned.1.call-done) | copy-start | bytes 1572868
  1442.7 40.3 %copy-start.119 = (bf16[128,2304]{1,0:T(8,128)(2,1)S(1)}, bf16[128,2304]{1,0:T(8,128)(2,1)}, u32[]{:S(2)}) copy-start(bf16[128,2304]{1,0:T(8,128)(2,1)} %all-reduce.76.cloned.1.call-done) | copy-start | bytes 1769476
  1442.7 41.0 %collective-permute-start.15 = (bf16[128,2048]{1,0:T(8,128)(2,1)}, bf16[128,2048]{1,0:T(8,128)(2,1)}, u32[]{:S(2)}, u32[]{:S(2)}) collective-permute-start(bf16[128,2048]{1,0:T(8,128)(2,1)} %fusion.207), channel_id=1, source_target_pairs={{0,16},{16,0},{1,17},{17,1},{2,18},{18,2},{3,19},{19,3},{4,20},{20... | collective-permute-start | bytes 1572872 | tf_op jit(solution)/shard_map/ppermute | solution.py:463
  1444.1 39.7 %copy-start.143 = (bf16[128,2048]{1,0:T(8,128)(2,1)S(1)}, bf16[128,2048]{1,0:T(8,128)(2,1)}, u32[]{:S(2)}) copy-start(bf16[128,2048]{1,0:T(8,128)(2,1)} %all-reduce.80.cloned.1.call-done) | copy-start | bytes 1572868
  1483.3 3.3 collective-permute-start.16
  (432 other events, 2729.3 us)
Sparse Core Ops, SparseCore 0:
  12.9 41.5 all-gather.14
  93.7 44.7 all-gather.26
  140.4 35.4 all-gather.16
  177.6 36.7 all-gather.18
  216.1 38.9 all-gather.20
  293.2 45.1 all-gather.28
  340.3 35.6 all-gather.22
  377.8 36.7 all-gather.24
  483.7 45.9 all-gather.30
  681.2 34.4 reduce-scatter.16
  721.5 44.9 all-gather.32
  769.6 33.8 reduce-scatter.14
  805.9 38.4 all-reduce.71
  847.3 37.3 reduce-scatter.12
  903.1 37.4 all-reduce.73
  946.5 122.9 all-reduce.67
  1071.7 40.0 all-reduce.75
  1115.2 34.8 reduce-scatter.10
  1156.5 123.0 all-reduce.69
  1283.3 36.0 reduce-scatter.8
  1321.7 38.2 all-reduce.77
  1363.6 37.3 reduce-scatter.6
  1403.4 38.2 all-reduce.79
  1443.9 39.0 all-reduce.81

commit v3 on v2

--- a/solution.py
+++ b/solution.py
@@ -556,9 +556,7 @@
 
     final = {}
     parts = [dict() for _ in range(sections)]
-    sums = [None] * sections
     before = None
-    sum_before = None
     for level in reversed(range(sections)):
         for at in (10, 1, 2):
             scattered = scatter_large(totals[level][at])
@@ -568,24 +566,33 @@
                 )
             parts[level][at] = lax.psum(scattered, "seq")
             before = (level, at)
-        flat = jnp.concatenate([totals[level][at].reshape(-1) for at, _ in SMALL])
-        if sum_before is not None:
-            flat, sums[sum_before] = lax.optimization_barrier((flat, sums[sum_before]))
-        sums[level] = lax.psum(flat, ("section", "wa", "seq"))
-        sum_before = level
     for at in LARGE:
         stacked = jnp.stack([parts[level][at] for level in range(sections)])
         got = swapped(stacked, rank, sections)
         final[at] = jnp.concatenate(got, axis=0).astype(jnp.float32)[None]
-    flat = lax.dynamic_index_in_dim(jnp.stack(sums), rank, 0, False)
+    count = lax.axis_size("wa")
+    rows = []
+    for level in range(sections):
+        cuts = []
+        for at, axis in SMALL:
+            value = totals[level][at]
+            if axis == 2:
+                value = jnp.moveaxis(value.reshape(value.shape[0], count, -1), 1, 0)
+            cuts.append(value.reshape(count, -1))
+        row = jnp.concatenate(cuts, axis=1)
+        rows.append(jnp.pad(row, ((0, 0), (0, -row.shape[1] % 2048))).reshape(-1, 128))
+    got = swapped(jnp.stack(rows), rank, sections)
+    mine = got[0]
+    for piece in got[1:]:
+        mine = mine + piece
+    mine = lax.psum_scatter(mine, "wa", scatter_dimension=0, tiled=True)
+    flat = lax.psum(mine, "seq").reshape(-1)
     start = 0
     for at, axis in SMALL:
-        shape = totals[0][at].shape
-        size = totals[0][at].size
-        whole = flat[start : start + size].reshape(shape)
+        shape = shards[at].shape
+        size = shards[at].size
+        final[at] = flat[start : start + size].reshape(shape)
         start += size
-        length = shards[at].shape[axis]
-        final[at] = lax.dynamic_slice_in_dim(whole, wa_rank * length, length, axis - 1)[None]
     return (layer_out, input_grad) + tuple(final[at] for at in range(len(shards)))
 
 

time: 1510 us -> 1280 us (0.85)
  waiting for transfers between devices: 659 us -> 411 us
  blocking collectives: 10.6 us -> 30.6 us
    psum x2 -> x0, waiting for transfers between devices: 246 us -> none  [on_device(): sums[level] = lax.psum(flat, ('section', 'wa', 'seq'))]
    psum x0 -> x1, blocking collectives: none -> 19.9 us  [on_device(): flat = lax.psum(mine, 'seq').reshape(-1)]
    reduce_scatter x6, waiting for transfers between devices: 106 us -> 88.5 us  [scatter_large(): return lax.psum_scatter(total, 'wa', scatter_dimension=0, tiled=True)]
    unnamed x915 -> x913, local copies, waits for them, and re-layouts: 38.7 us -> 39.6 us
  transfers between devices with their start and end apart: 42 -> 42, of which waited for: 22 -> 22; matrix products, arithmetic and copies ran while one was open for 35% -> 41% of each run, Pallas kernels for 0% -> 0%
where the time goes in v3:
time: 1280 us; the launch traced here: 1260 us
  waiting for transfers between devices  411 us (32%)
  matrix products  283 us (22%)
  local copies, waits for them, and re-layouts  253 us (20%)
  other arithmetic  250 us (20%)
  blocking collectives  30.6 us (2%)
  between operations  19.7 us (2%)
  starting transfers between devices  14.7 us (1%)
    psum x6, waiting for transfers between devices, on_device(): parts[level][at] = lax.psum(scattered, 'seq')  176 us
    all_gather x6, waiting for transfers between devices, fetch_large(): lax.all_gather(pieces[level], ('wa', 'section'), axis=0, tiled=True)  116 us
    reduce_scatter x6, waiting for transfers between devices, scatter_large(): return lax.psum_scatter(total, 'wa', scatter_dimension=0, tiled=True)  88.5 us
    unnamed x913, local copies, waits for them, and re-layouts  39.6 us
    dot_general x24, matrix products, block_piece(): fresh_state = jnp.einsum('sd,sn->dn', scaled, keys_in, precision=HIGHEST)  37.7 us
    dot_general x24, matrix products, reach_piece(): reach_mat = jnp.einsum('tn,dn->td', queries, start_state, precision=HIGHEST)  36.5 us
    dot_general x8, matrix products, layer_back(): jnp.einsum('thp,shp->hts', grad_heads, heads_view, preferred_element_type...  30.4 us
    dot_general x24, matrix products, block_piece(): gram_mat = jnp.einsum('tn,sn->ts', queries, keys_in, precision=HIGHEST)  26.6 us
  transfers between devices with their start and end apart: 42, of which 22 were waited for; matrix products, arithmetic and copies ran while one was open for 41% of the time, Pallas kernels for 0%

profile of v3, /device:TPU:0, one launch (start us, length us, event | category | flops | bytes accessed | tf_op | source)
XLA Modules:
  0.0 1261.8 jit_solution(14304775140717311743)
XLA Ops:
  13.4 10.6 all_gather.41
  33.0 21.4 %all-gather.15.cloned.1.call-done = bf16[1024,2304]{1,0:T(8,128)(2,1)} async-done(((bf16[128,2304]{1,0:T(8,128)(2,1)}), bf16[1024,2304]{1,0:T(8,128)(2,1)}) %all-gather.15.cloned.1.call-update) | async-done | bytes 4718608 | tf_op jit(solution)/shard_map/all_gather | solution.py:450
  54.4 5.3 convolution_convert_fusion.3
  61.9 4.0 collective-permute-start.1
  79.5 4.5 fusion.404
  162.2 4.0 fusion.89
  177.9 12.4 multiply_reduce_fusion.19
  190.3 24.1 %all-gather.19.cloned.1.call-done = bf16[2048,1024]{1,0:T(8,128)(2,1)} async-done(((bf16[256,1024]{1,0:T(8,128)(2,1)}), bf16[2048,1024]{1,0:T(8,128)(2,1)}) %all-gather.19.cloned.1.call-update) | async-done | bytes 4194320 | tf_op jit(solution)/shard_map/all_gather | solution.py:450
  214.4 6.2 fusion.44
  225.4 29.6 %all-gather.21.cloned.1.call-done = bf16[1024,2304]{1,0:T(8,128)(2,1)} async-done(((bf16[128,2304]{1,0:T(8,128)(2,1)}), bf16[1024,2304]{1,0:T(8,128)(2,1)}) %all-gather.21.cloned.1.call-update) | async-done | bytes 4718608 | tf_op jit(solution)/shard_map/all_gather | solution.py:450
  255.1 5.3 convolution_convert_fusion.2
  275.8 4.6 fusion.399
  287.3 5.7 concatenate.132
  332.7 5.5 all-gather.29.cloned.1.call-done
  340.3 3.4 fusion.102
  343.8 3.6 maximum_add_fusion.3
  357.3 18.5 %all-gather.23.cloned.1.call-done = bf16[1024,2048]{1,0:T(8,128)(2,1)} async-done(((bf16[128,2048]{1,0:T(8,128)(2,1)}), bf16[1024,2048]{1,0:T(8,128)(2,1)}) %all-gather.23.cloned.1.call-update) | async-done | bytes 4194320 | tf_op jit(solution)/shard_map/all_gather | solution.py:450
  375.9 10.0 multiply_reduce_fusion.18
  387.8 4.5 convolution_convert_fusion.7
  392.3 22.2 %all-gather.25.cloned.1.call-done = bf16[2048,1024]{1,0:T(8,128)(2,1)} async-done(((bf16[256,1024]{1,0:T(8,128)(2,1)}), bf16[2048,1024]{1,0:T(8,128)(2,1)}) %all-gather.25.cloned.1.call-update) | async-done | bytes 4194320 | tf_op jit(solution)/shard_map/all_gather | solution.py:450
  414.5 7.3 multiply_reduce_fusion.13
  421.9 6.2 multiply_reduce_fusion.14
  430.8 4.5 convolution_convert_fusion.6
  469.9 3.5 slice_multiply_fusion.30
  477.9 5.7 multiply_reduce_fusion.15
  524.4 10.1 fusion.71
  541.2 4.8 multiply_reduce_fusion.42
  589.1 8.9 slice_multiply_fusion.6
  623.9 11.4 multiply_reduce_fusion.7
  635.3 7.4 broadcast_multiply_fusion
  657.0 3.6 fusion.34
  661.2 4.9 convolution_convert_fusion.1
  668.2 8.9 multiply_reduce_fusion.8
  677.2 3.9 fusion.16
  681.2 11.9 multiply_reduce_fusion.9
  701.0 4.4 convolution_convert_fusion.4
  705.5 4.5 convolution_convert_fusion.5
  717.9 3.5 multiply_reduce_fusion.10
  721.9 6.0 slice_multiply_fusion.22
  753.8 3.7 fusion.17
  783.5 8.1 fusion.79
  798.3 4.4 fusion.6
  804.0 5.3 multiply_reduce_fusion.38
  830.2 5.7 slice_multiply_fusion.14
  838.7 11.1 multiply_reduce_fusion.3
  849.8 7.5 broadcast_multiply_fusion.4
  881.1 4.0 collective-permute-done.7
  885.1 6.8 fusion.221
  896.7 4.7 convolution_convert_fusion
  902.9 37.5 %all-reduce.70.cloned.1.call-done = bf16[128,2048]{1,0:T(8,128)(2,1)} async-done(((bf16[128,2048]{1,0:T(8,128)(2,1)}), bf16[128,2048]{1,0:T(8,128)(2,1)}) %all-reduce.70.cloned.1.call-update) | async-done | bytes 524304 | tf_op jit(solution)/shard_map/psum | solution.py:567
  940.5 4.5 fusion.18
  953.7 4.5 fusion.19
  961.9 19.9 %all-reduce.72.cloned.1.call-done = bf16[128,2304]{1,0:T(8,128)(2,1)} async-done(((bf16[128,2304]{1,0:T(8,128)(2,1)}), bf16[128,2304]{1,0:T(8,128)(2,1)}) %all-reduce.72.cloned.1.call-update) | async-done | bytes 589840 | tf_op jit(solution)/shard_map/psum | solution.py:567
  981.8 38.3 %reduce-scatter.14.cloned.1.call-done = bf16[256,1024]{1,0:T(8,128)(2,1)} async-done(((bf16[1024,1024]{1,0:T(8,128)(2,1)}), bf16[256,1024]{1,0:T(8,128)(2,1)}) %reduce-scatter.14.cloned.1.call-update) | async-done | bytes 524304 | tf_op jit(solution)/shard_map/reduce_scatter | solution.py:485
  1020.2 4.3 fusion.7
  1025.7 5.8 fusion.69
  1036.7 10.3 reduce-scatter.8.cloned.1.call-done
  1046.9 19.9 %psum.49 = f32[96,128]{1,0:T(8,128)S(1)} all-reduce(f32[96,128]{1,0:T(8,128)} %reduce-scatter.8.cloned.1.call-done), channel_id=1, replica_groups=mesh['section'=2,'seq'=4,'wa'=4] {'seq'}, use_global_device_ids=true, to_apply=%region_133.135 | all-reduce | flops 12288 | bytes 98304 | tf_op jit(solution)/shard_map/psum | solution.py:589
  1070.7 15.3 %reduce-scatter.12.cloned.1.call-done = bf16[128,2048]{1,0:T(8,128)(2,1)} async-done(((bf16[512,2048]{1,0:T(8,128)(2,1)}), bf16[128,2048]{1,0:T(8,128)(2,1)}) %reduce-scatter.12.cloned.1.call-update) | async-done | bytes 524304 | tf_op jit(solution)/shard_map/reduce_scatter | solution.py:485
  1086.0 40.5 %all-reduce.74.cloned.1.call-done = bf16[256,1024]{1,0:T(8,128)(2,1)} async-done(((bf16[256,1024]{1,0:T(8,128)(2,1)}), bf16[256,1024]{1,0:T(8,128)(2,1)}) %all-reduce.74.cloned.1.call-update) | async-done | bytes 524304 | tf_op jit(solution)/shard_map/psum | solution.py:567
  1126.9 3.4 convert_select_fusion.1
  1132.6 35.0 %reduce-scatter.10.cloned.1.call-done = bf16[128,2304]{1,0:T(8,128)(2,1)} async-done(((bf16[512,2304]{1,0:T(8,128)(2,1)}), bf16[128,2304]{1,0:T(8,128)(2,1)}) %reduce-scatter.10.cloned.1.call-update) | async-done | bytes 589840 | tf_op jit(solution)/shard_map/reduce_scatter | solution.py:485
  1167.6 40.6 %all-reduce.76.cloned.1.call-done = bf16[128,2048]{1,0:T(8,128)(2,1)} async-done(((bf16[128,2048]{1,0:T(8,128)(2,1)}), bf16[128,2048]{1,0:T(8,128)(2,1)}) %all-reduce.76.cloned.1.call-update) | async-done | bytes 524304 | tf_op jit(solution)/shard_map/psum | solution.py:567
  1212.2 37.5 %all-reduce.78.cloned.1.call-done = bf16[1,128,2304]{2,1,0:T(8,128)(2,1)} async-done(((bf16[1,128,2304]{2,1,0:T(8,128)(2,1)}), bf16[1,128,2304]{2,1,0:T(8,128)(2,1)}) %all-reduce.78.cloned.1.call-update) | async-done | bytes 589840 | tf_op jit(solution)/shard_map/psum | solution.py:567
  (1586 shorter events, 536.4 us)
Async XLA Ops:
  7.3 47.2 %all-gather.15.cloned.1.call-start = ((), (), s32[]{:S(2)}) async-start(), calls=%async_computation.7 | async-start | bytes 5308416 | tf_op jit(solution)/shard_map/all_gather | solution.py:450
  8.4 2.1 collective-permute-start
  12.8 147.3 %all-gather.27.cloned.1.call-start = ((), (), s32[]{:S(2)}) async-start(), calls=%async_computation.26 | async-start | bytes 2641920 | tf_op jit(solution)/shard_map/all_gather | solution.py:101
  32.3 77.7 %copy-start.183 = (f32[1,32]{0,1:T(8,128)}, f32[1,32]{0,1:T(8,128)S(1)}, u32[]{:S(2)}) copy-start(f32[1,32]{0,1:T(8,128)S(1)} %get-tuple-element.324) | copy-start | bytes 388
  61.9 15.3 %collective-permute-start.1 = (bf16[3,2304]{1,0:T(4,128)(2,1)}, bf16[3,2304]{1,0:T(4,128)(2,1)}, u32[]{:S(2)}, u32[]{:S(2)}) collective-permute-start(bf16[3,2304]{1,0:T(4,128)(2,1)} %slice.903), channel_id=1, source_target_pairs={{0,4},{4,8},{8,12},{1,5},{5,9},{9,13},{2,6},{6,10},{10,14},{3,7},{... | collective-permute-start | bytes 41480 | tf_op jit(solution)/shard_map/ppermute | solution.py:17
  86.0 80.3 %copy-start.21 = (f32[2048,128]{1,0:T(8,128)}, f32[2048,128]{1,0:T(8,128)S(1)}, u32[]{:S(2)}) copy-start(f32[2048,128]{1,0:T(8,128)S(1)} %convolution_add_fusion.7) | copy-start | bytes 3145732
  93.6 84.3 %all-gather.17.cloned.1.call-start = ((), (), s32[]{:S(2)}) async-start(), calls=%async_computation.8 | async-start | bytes 4718592 | tf_op jit(solution)/shard_map/all_gather | solution.py:450
  94.9 2.0 collective-permute-start.2
  98.1 116.3 %all-gather.19.cloned.1.call-start = ((), (), s32[]{:S(2)}) async-start(), calls=%async_computation.9 | async-start | bytes 4718592 | tf_op jit(solution)/shard_map/all_gather | solution.py:450
  98.2 2.0 collective-permute-start.3
  101.3 153.8 %all-gather.21.cloned.1.call-start = ((), (), s32[]{:S(2)}) async-start(), calls=%async_computation.10 | async-start | bytes 5308416 | tf_op jit(solution)/shard_map/all_gather | solution.py:450
  109.9 44.6 %copy-start.326 = (f32[32,128]{1,0:T(8,128)}, f32[32,128]{1,0:T(8,128)S(1)}, u32[]{:S(2)}) copy-start(f32[32,128]{1,0:T(8,128)S(1)} %copy.575) | copy-start | bytes 49156
  110.4 55.9 %copy-start.168 = (f32[4,2048]{1,0:T(4,128)}, f32[4,2048]{1,0:T(4,128)S(1)}, u32[]{:S(2)}) copy-start(f32[4,2048]{1,0:T(4,128)S(1)} %mul.1700) | copy-start | bytes 98308
  110.9 61.9 %copy-start.24 = (f32[128,2048]{1,0:T(8,128)}, f32[128,2048]{1,0:T(8,128)S(1)}, u32[]{:S(2)}) copy-start(f32[128,2048]{1,0:T(8,128)S(1)} %copy.611) | copy-start | bytes 3145732
  114.2 61.0 %copy-start.26 = (f32[128,2048]{1,0:T(8,128)}, f32[128,2048]{1,0:T(8,128)S(1)}, u32[]{:S(2)}) copy-start(f32[128,2048]{1,0:T(8,128)S(1)} %copy.609) | copy-start | bytes 3145732
  121.6 39.9 %copy-start.411 = (pred[4]{0:T(512)(128)(4,1)}, pred[4]{0:T(512)(128)(4,1)S(1)}, u32[]{:S(2)}) copy-start(pred[4]{0:T(512)(128)(4,1)S(1)} %get-tuple-element.544) | copy-start | bytes 16
  122.2 38.7 %copy-start.405 = (pred[4,4]{1,0:T(4,128)(4,1)}, pred[4,4]{1,0:T(4,128)(4,1)S(1)}, u32[]{:S(2)}) copy-start(pred[4,4]{1,0:T(4,128)(4,1)S(1)} %fusion.333) | copy-start | bytes 52
  122.2 38.7 %copy-start.407 = (pred[4,4]{1,0:T(4,128)(4,1)}, pred[4,4]{1,0:T(4,128)(4,1)S(1)}, u32[]{:S(2)}) copy-start(pred[4,4]{1,0:T(4,128)(4,1)S(1)} %fusion.332) | copy-start | bytes 52
  122.9 91.5 %copy-start.291 = (f32[1,4,512]{2,0,1:T(1,128)}, f32[1,4,512]{2,0,1:T(1,128)S(1)}, u32[]{:S(2)}) copy-start(f32[1,4,512]{2,0,1:T(1,128)S(1)} %get-tuple-element.396) | copy-start | bytes 24580
  122.9 215.3 %all-gather.29.cloned.1.call-start = ((), (), s32[]{:S(2)}) async-start(), calls=%async_computation.27 | async-start | bytes 2641920 | tf_op jit(solution)/shard_map/all_gather | solution.py:101
  220.6 39.7 %copy-start.78 = (bf16[512,1024]{1,0:T(8,128)(2,1)}, bf16[512,1024]{1,0:T(8,128)(2,1)S(1)}, u32[]{:S(2)}) copy-start(bf16[512,1024]{1,0:T(8,128)(2,1)S(1)} %get-tuple-element.527) | copy-start | bytes 3145732
  220.6 39.7 %copy-start.367 = (f32[512]{0:T(512)}, f32[512]{0:T(512)S(1)}, u32[]{:S(2)}) copy-start(f32[512]{0:T(512)S(1)} %fusion.336) | copy-start | bytes 6148
  222.3 38.1 %copy-start.175 = (f32[512,32]{0,1:T(8,128)}, f32[512,32]{0,1:T(8,128)S(1)}, u32[]{:S(2)}) copy-start(f32[512,32]{0,1:T(8,128)S(1)} %get-tuple-element.425) | copy-start | bytes 196612
  222.9 37.5 %copy-start.163 = (f32[128,32]{1,0:T(8,128)}, f32[128,32]{1,0:T(8,128)S(1)}, u32[]{:S(2)}) copy-start(f32[128,32]{1,0:T(8,128)S(1)} %reduce_window_sum.84) | copy-start | bytes 49156
  223.2 37.2 %copy-start.164 = (f32[128,32]{1,0:T(8,128)}, f32[128,32]{1,0:T(8,128)S(1)}, u32[]{:S(2)}) copy-start(f32[128,32]{1,0:T(8,128)S(1)} %reduce_window_sum.83) | copy-start | bytes 49156
  225.4 39.9 %copy-start.416 = (bf16[64]{0:T(256)(128)(2,1)S(1)}, bf16[64]{0:T(256)(128)(2,1)}, u32[]{:S(2)}) copy-start(bf16[64]{0:T(256)(128)(2,1)} %copy-done.415) | copy-start | bytes 388
  262.0 11.6 collective-permute-start.4
  293.0 82.8 %all-gather.23.cloned.1.call-start = ((), (), s32[]{:S(2)}) async-start(), calls=%async_computation.11 | async-start | bytes 4718592 | tf_op jit(solution)/shard_map/all_gather | solution.py:450
  293.7 120.7 %all-gather.25.cloned.1.call-start = ((), (), s32[]{:S(2)}) async-start(), calls=%async_computation.12 | async-start | bytes 4718592 | tf_op jit(solution)/shard_map/all_gather | solution.py:450
  295.3 245.8 %all-gather.31.cloned.1.call-start = ((), (), s32[]{:S(2)}) async-start(), calls=%async_computation.28 | async-start | bytes 2621440 | tf_op jit(solution)/shard_map/all_gather | solution.py:330
  483.5 314.6 %reduce-scatter.20.cloned.1.call-start = ((), (), s32[]{:S(2)}) async-start(), calls=%async_computation.19 | async-start | bytes 2621440 | tf_op jit(solution)/shard_map/reduce_scatter | solution.py:485
  648.4 5.9 collective-permute-start.6
  661.2 44.3 %copy-start.14 = (f32[512,1024]{1,0:T(8,128)}, f32[512,1024]{1,0:T(8,128)S(1)}, u32[]{:S(2)}) copy-start(f32[512,1024]{1,0:T(8,128)S(1)} %fusion.42) | copy-start | bytes 6291460
  667.6 9.6 collective-permute-start.15
  681.1 121.9 %all-gather.33.cloned.1.call-start = ((), (), s32[]{:S(2)}) async-start(), calls=%async_computation.29 | async-start | bytes 2621440 | tf_op jit(solution)/shard_map/all_gather | solution.py:330
  697.1 56.7 %collective-permute-start.14 = (bf16[4,128,2048]{2,1,0:T(8,128)(2,1)}, bf16[4,128,2048]{2,1,0:T(8,128)(2,1)}, u32[]{:S(2)}, u32[]{:S(2)}) collective-permute-start(bf16[4,128,2048]{2,1,0:T(8,128)(2,1)} %dynamic-slice_bitcast_fusion.3), channel_id=1, source_target_pairs={{0,16},{16,0},{1,17},{17,1},{2,18},{18,2},{3,19},{19,3},{4,20},{20... | collective-permute-start | bytes 6291464 | tf_op jit(solution)/shard_map/ppermute | solution.py:482
  700.9 97.4 %collective-permute-start.13 = (bf16[4,128,2304]{2,1,0:T(8,128)(2,1)}, bf16[4,128,2304]{2,1,0:T(8,128)(2,1)}, u32[]{:S(2)}, u32[]{:S(2)}) collective-permute-start(bf16[4,128,2304]{2,1,0:T(8,128)(2,1)} %dynamic-slice_bitcast_fusion), channel_id=1, source_target_pairs={{0,16},{16,0},{1,17},{17,1},{2,18},{18,2},{3,19},{19,3},{4,20},{20... | collective-permute-start | bytes 7077896 | tf_op jit(solution)/shard_map/ppermute | solution.py:482
  721.4 181.4 %reduce-scatter.18.cloned.1.call-start = ((), (), s32[]{:S(2)}) async-start(), calls=%async_computation.18 | async-start | bytes 2621440 | tf_op jit(solution)/shard_map/reduce_scatter | solution.py:485
  757.5 145.3 %all-reduce.68.cloned.1.call-start = ((), (), s32[]{:S(2)}) async-start(), calls=%async_computation.20 | async-start | bytes 1048576 | tf_op jit(solution)/shard_map/psum | solution.py:567
  798.2 104.7 %reduce-scatter.16.cloned.1.call-start = ((), (), s32[]{:S(2)}) async-start(), calls=%async_computation.17 | async-start | bytes 2949120 | tf_op jit(solution)/shard_map/reduce_scatter | solution.py:485
  802.8 137.7 %all-reduce.70.cloned.1.call-start = ((), (), s32[]{:S(2)}) async-start(), calls=%async_computation.21 | async-start | bytes 1048576 | tf_op jit(solution)/shard_map/psum | solution.py:567
  879.2 5.9 collective-permute-start.7
  902.8 37.7 %collective-permute-start.12 = (bf16[4,256,1024]{2,1,0:T(8,128)(2,1)}, bf16[4,256,1024]{2,1,0:T(8,128)(2,1)}, u32[]{:S(2)}, u32[]{:S(2)}) collective-permute-start(bf16[4,256,1024]{2,1,0:T(8,128)(2,1)} %dynamic-slice_bitcast_fusion.4), channel_id=1, source_target_pairs={{0,16},{16,0},{1,17},{17,1},{2,18},{18,2},{3,19},{19,3},{4,20},{20... | collective-permute-start | bytes 6291464 | tf_op jit(solution)/shard_map/ppermute | solution.py:482
  902.9 78.9 %all-reduce.72.cloned.1.call-start = ((), (), s32[]{:S(2)}) async-start(), calls=%async_computation.22 | async-start | bytes 1179648 | tf_op jit(solution)/shard_map/psum | solution.py:567
  940.5 79.6 %reduce-scatter.14.cloned.1.call-start = ((), (), s32[]{:S(2)}) async-start(), calls=%async_computation.16 | async-start | bytes 2621440 | tf_op jit(solution)/shard_map/reduce_scatter | solution.py:485
  945.2 101.7 %reduce-scatter.8.cloned.1.call-start = ((), (), s32[]{:S(2)}) async-start(), calls=%async_computation.13 | async-start | bytes 245760 | tf_op jit(solution)/shard_map/reduce_scatter | solution.py:588
  948.5 5.3 collective-permute-start.11
  951.3 1.6 collective-permute-start.9
  953.7 132.3 %reduce-scatter.12.cloned.1.call-start = ((), (), s32[]{:S(2)}) async-start(), calls=%async_computation.15 | async-start | bytes 2621440 | tf_op jit(solution)/shard_map/reduce_scatter | solution.py:485
  958.2 168.3 %all-reduce.74.cloned.1.call-start = ((), (), s32[]{:S(2)}) async-start(), calls=%async_computation.23 | async-start | bytes 1048576 | tf_op jit(solution)/shard_map/psum | solution.py:567
  961.5 58.6 %collective-permute-start.10 = (bf16[4,128,2304]{2,1,0:T(8,128)(2,1)}, bf16[4,128,2304]{2,1,0:T(8,128)(2,1)}, u32[]{:S(2)}, u32[]{:S(2)}) collective-permute-start(bf16[4,128,2304]{2,1,0:T(8,128)(2,1)} %dynamic-slice_bitcast_fusion.1), channel_id=1, source_target_pairs={{0,16},{16,0},{1,17},{17,1},{2,18},{18,2},{3,19},{19,3},{4,20},{20... | collective-permute-start | bytes 7077896 | tf_op jit(solution)/shard_map/ppermute | solution.py:482
  1020.1 147.5 %reduce-scatter.10.cloned.1.call-start = ((), (), s32[]{:S(2)}) async-start(), calls=%async_computation.14 | async-start | bytes 2949120 | tf_op jit(solution)/shard_map/reduce_scatter | solution.py:485
  1024.5 183.7 %all-reduce.76.cloned.1.call-start = ((), (), s32[]{:S(2)}) async-start(), calls=%async_computation.24 | async-start | bytes 1048576 | tf_op jit(solution)/shard_map/psum | solution.py:567
  1032.0 2.7 collective-permute-start.5
  1034.4 92.5 %collective-permute-start.8 = (bf16[1,512,1024]{2,1,0:T(8,128)(2,1)}, bf16[1,512,1024]{2,1,0:T(8,128)(2,1)}, u32[]{:S(2)}, u32[]{:S(2)}) collective-permute-start(bf16[1,512,1024]{2,1,0:T(8,128)(2,1)} %fusion.132), channel_id=1, source_target_pairs={{0,16},{16,0},{1,17},{17,1},{2,18},{18,2},{3,19},{19,3},{4,20},{20... | collective-permute-start | bytes 3145736 | tf_op jit(solution)/shard_map/ppermute | solution.py:606
  1035.1 91.4 %copy-start.134 = (bf16[256,1024]{1,0:T(8,128)(2,1)S(1)}, bf16[256,1024]{1,0:T(8,128)(2,1)}, u32[]{:S(2)}) copy-start(bf16[256,1024]{1,0:T(8,128)(2,1)} %all-reduce.68.cloned.1.call-done) | copy-start | bytes 1572868
  1126.7 82.5 %collective-permute-start.18 = (bf16[256,1024]{1,0:T(8,128)(2,1)S(1)}, bf16[256,1024]{1,0:T(8,128)(2,1)}, u32[]{:S(2)}, u32[]{:S(2)}) collective-permute-start(bf16[256,1024]{1,0:T(8,128)(2,1)S(1)} %fusion.203), channel_id=1, source_target_pairs={{0,16},{16,0},{1,17},{17,1},{2,18},{18,2},{3,19},{19,3},{4,20},{20... | collective-permute-start | bytes 1572872 | tf_op jit(solution)/shard_map/ppermute | solution.py:463
  1126.8 122.9 %all-reduce.78.cloned.1.call-start = ((), (), s32[]{:S(2)}) async-start(), calls=%async_computation.25 | async-start | bytes 1179648 | tf_op jit(solution)/shard_map/psum | solution.py:567
  1130.3 78.0 %copy-start.135 = (bf16[128,2048]{1,0:T(8,128)(2,1)S(1)}, bf16[128,2048]{1,0:T(8,128)(2,1)}, u32[]{:S(2)}) copy-start(bf16[128,2048]{1,0:T(8,128)(2,1)} %all-reduce.70.cloned.1.call-done) | copy-start | bytes 1572868
  1132.6 76.6 %copy-start.139 = (bf16[256,1024]{1,0:T(8,128)(2,1)S(1)}, bf16[256,1024]{1,0:T(8,128)(2,1)}, u32[]{:S(2)}) copy-start(bf16[256,1024]{1,0:T(8,128)(2,1)} %all-reduce.74.cloned.1.call-done) | copy-start | bytes 1572868
  1209.2 40.4 %copy-start.118 = (bf16[128,2304]{1,0:T(8,128)(2,1)S(1)}, bf16[128,2304]{1,0:T(8,128)(2,1)}, u32[]{:S(2)}) copy-start(bf16[128,2304]{1,0:T(8,128)(2,1)} %all-reduce.72.cloned.1.call-done) | copy-start | bytes 1769476
  1209.2 41.2 %collective-permute-start.16 = (bf16[128,2048]{1,0:T(8,128)(2,1)}, bf16[128,2048]{1,0:T(8,128)(2,1)}, u32[]{:S(2)}, u32[]{:S(2)}) collective-permute-start(bf16[128,2048]{1,0:T(8,128)(2,1)} %fusion.207), channel_id=1, source_target_pairs={{0,16},{16,0},{1,17},{17,1},{2,18},{18,2},{3,19},{19,3},{4,20},{20... | collective-permute-start | bytes 1572872 | tf_op jit(solution)/shard_map/ppermute | solution.py:463
  1210.6 39.8 %copy-start.142 = (bf16[128,2048]{1,0:T(8,128)(2,1)S(1)}, bf16[128,2048]{1,0:T(8,128)(2,1)}, u32[]{:S(2)}) copy-start(bf16[128,2048]{1,0:T(8,128)(2,1)} %all-reduce.76.cloned.1.call-done) | copy-start | bytes 1572868
  1249.9 3.3 collective-permute-start.17
  (430 other events, 2726.3 us)
Sparse Core Ops, SparseCore 0:
  12.9 41.5 all-gather.14
  93.7 44.7 all-gather.26
  140.4 35.4 all-gather.16
  177.6 36.7 all-gather.18
  216.1 38.9 all-gather.20
  293.1 45.0 all-gather.28
  340.1 35.6 all-gather.22
  377.7 36.7 all-gather.24
  483.7 45.9 all-gather.30
  681.2 34.4 reduce-scatter.19
  721.5 44.9 all-gather.32
  769.6 33.9 reduce-scatter.17
  805.9 38.4 all-reduce.67
  847.3 37.3 reduce-scatter.15
  903.0 37.4 all-reduce.69
  942.7 39.0 all-reduce.71
  985.2 34.8 reduce-scatter.13
  1022.9 23.9 reduce-scatter.7
  1050.8 35.2 reduce-scatter.11
  1088.2 38.2 all-reduce.73
  1130.1 37.3 reduce-scatter.9
  1169.9 38.2 all-reduce.75
  1210.6 39.0 all-reduce.77
